TPU v7x, 32 devices: a whole 2x2x4 slice. The times are simulated.
32 devices in a mesh: row: 16 (over z, x, core), col: 2 (over y).
Axes of the slice: x: 2, y: 2, z: 4, core: 2. Of those that a mesh axis runs over, the one named last changes fastest.
Arguments:
- tokens: bfloat16 [27696, 1024], P('row', 'col'), may hold values from -80 to 80
- cotangent: bfloat16 [27696, 1024], P('row', 'col'), may hold values from -80 to 80
- ln1_gain: float32 [1024], replicated, may hold values from 0.2 to 4
- ln1_bias: float32 [1024], replicated, may hold values from -3 to 3
- ln2_gain: float32 [1024], replicated, may hold values from 0.2 to 4
- ln2_bias: float32 [1024], replicated, may hold values from -3 to 3
- w_qkv: bfloat16 [3, 1024, 1024], P(None, 'row', 'col'), may hold values from -0.1875 to 0.1875
- qv_bias: float32 [2, 1024], P(None, 'col'), may hold values from -3 to 3
- w_out: bfloat16 [1024, 1024], P('col', 'row'), may hold values from -0.75 to 0.75
- out_bias: float32 [1024], replicated, may hold values from -3 to 3
- w_up: bfloat16 [1024, 4096], P('row', 'col'), may hold values from -0.1875 to 0.1875
- up_bias: float32 [4096], P('col'), may hold values from -3 to 3
- w_down: bfloat16 [4096, 1024], P('col', 'row'), may hold values from -0.1875 to 0.1875
- down_bias: float32 [1024], replicated, may hold values from -3 to 3
- adapter_ids: int32 [48], P('row'), may hold values from 0 to 7
- a_qkv: bfloat16 [1024, 384], replicated, may hold values from -0.1875 to 0.1875
- b_qkv: bfloat16 [3, 128, 1024], P(None, None, 'col'), may hold values from -0.75 to 0.75
- a_out: bfloat16 [1024, 128], P('col'), may hold values from -0.1875 to 0.1875
- b_out: bfloat16 [128, 1024], replicated, may hold values from -0.75 to 0.75
- a_up: bfloat16 [1024, 128], replicated, may hold values from -0.1875 to 0.1875
- b_up: bfloat16 [128, 4096], P(None, 'col'), may hold values from -0.75 to 0.75
- a_down: bfloat16 [4096, 128], P('col'), may hold values from -0.09375 to 0.09375
- b_down: bfloat16 [128, 1024], replicated, may hold values from -0.75 to 0.75
Outputs:
- layer_out: bfloat16 [27696, 1024], P('row', 'col')
- tokens_grad: float32 [27696, 1024], P('row', 'col')
- grad_a_qkv: float32 [1024, 384], replicated
- grad_b_qkv: float32 [3, 128, 1024], P(None, None, 'col')
- grad_a_out: float32 [1024, 128], P('col')
- grad_b_out: float32 [128, 1024], replicated
- grad_a_up: float32 [1024, 128], replicated
- grad_b_up: float32 [128, 4096], P(None, 'col')
- grad_a_down: float32 [4096, 128], P('col')
- grad_b_down: float32 [128, 1024], replicated
Inputs may be any that keep to these rules, and one draw needn't show every extreme that they name: `adapter_ids`: each image's adapter number.
All inputs are finite; a program needn't handle non-finite values.
Results may differ from a plain program's by a relative error of at most 0.019.
The roundings to bfloat16 on the way count: a program that leaves them out, or rounds other values in their place, can miss the bound.
Values may be sent and summed in bfloat16 or wider, within the bound.
No kernel may reach another device: no remote copies, remote signals or barrier semaphores. Data moves between devices by JAX's collectives and lax.ppermute only.
A program may use at most 320 MiB of HBM per device.

v0:
```python
import jax
import jax.numpy as jnp
from jax import lax
from jax.sharding import PartitionSpec as P

HD = 64
RANK = 16


EPS = 1e-05
GELU_SCALE = 1.702


def column_sums(first, second):
    return lax.psum((first, second), "col")


def gather_features(values):
    return lax.all_gather(values, "col", axis=1, tiled=True)


def sum_partials(terms):
    return lax.psum_scatter(
        terms.astype(jnp.bfloat16), "col", scatter_dimension=1, tiled=True
    ).astype(jnp.float32)


def norm_split(values, feature_width):
    first, second = column_sums(jnp.sum(values, axis=1), jnp.sum(values * values, axis=1))
    centre = first / feature_width
    inverse = lax.rsqrt(second / feature_width - centre * centre + EPS)
    return ((values - centre[:, None]) * inverse[:, None], inverse)


def norm_back(grad_normed, normal_rows, inverse, gain_part, feature_width):
    scaled = grad_normed * gain_part
    first, second = column_sums(jnp.sum(scaled, axis=1), jnp.sum(scaled * normal_rows, axis=1))
    return inverse[:, None] * (
        scaled - first[:, None] / feature_width - normal_rows * second[:, None] / feature_width
    )


def select_rows(low_rank, onehot, image_len):
    image_count, stack_width = onehot.shape
    shaped = low_rank.reshape(image_count, image_len, -1, stack_width)
    return (shaped * onehot[:, None, None, :]).reshape(low_rank.shape).astype(jnp.bfloat16)


def mult(form, first, second):
    return jnp.einsum(form, first, second, preferred_element_type=jnp.float32)


def on_device(
    tokens,
    cotangent,
    ln1_gain,
    ln1_bias,
    ln2_gain,
    ln2_bias,
    w_qkv,
    qv_bias,
    w_out,
    out_bias,
    w_up,
    up_bias,
    w_down,
    down_bias,
    adapter_ids,
    a_qkv,
    b_qkv,
    a_out,
    b_out,
    a_up,
    b_up,
    a_down,
    b_down,
):
    row_count, part_width = tokens.shape
    feature_width = a_qkv.shape[0]
    stack_width = a_qkv.shape[1] // 3
    image_count = adapter_ids.shape[0]
    image_len = row_count // image_count
    head_count = part_width // HD
    scale = HD ** (-0.5)
    offset = lax.axis_index("col") * part_width

    def own_part(values, axis):
        return lax.dynamic_slice_in_dim(values, offset, part_width, axis)

    owners = lax.iota(jnp.int32, stack_width) // RANK
    onehot = (adapter_ids[:, None] == owners[None, :]).astype(jnp.float32)
    wide_qkv, wide_out, wide_up, wide_down = (
        lax.all_gather(w_qkv, "row", axis=1, tiled=True),
        lax.all_gather(w_out, "row", axis=1, tiled=True),
        lax.all_gather(w_up, "row", axis=0, tiled=True),
        lax.all_gather(w_down, "row", axis=1, tiled=True),
    )
    inputs = tokens.astype(jnp.float32)
    normal_one, inverse_one = norm_split(inputs, feature_width)
    normed_part = (normal_one * own_part(ln1_gain, 0) + own_part(ln1_bias, 0)).astype(jnp.bfloat16)
    normed_one = gather_features(normed_part)
    projected = mult("td,kde->kte", normed_one, wide_qkv)
    kept_qkv = select_rows(mult("td,dj->tj", normed_one, a_qkv), onehot, image_len)
    projected = projected + mult("tkj,kje->kte", kept_qkv.reshape(row_count, 3, stack_width), b_qkv)
    bias_rows = jnp.stack([qv_bias[0], jnp.zeros_like(qv_bias[0]), qv_bias[1]])[:, None, :]
    qkv = (projected + bias_rows).astype(jnp.bfloat16)
    shaped = qkv.reshape(3, image_count, image_len, head_count, HD)
    queries, key_rows, value_rows = (shaped[0], shaped[1], shaped[2])
    scores = mult("bqhd,bkhd->bhqk", queries, key_rows) * scale
    highest = jnp.max(scores, axis=-1, keepdims=True)
    log_total = highest + jnp.log(jnp.sum(jnp.exp(scores - highest), axis=-1, keepdims=True))
    weights_low = jnp.exp(scores - log_total).astype(jnp.bfloat16)
    attended = mult("bhqk,bkhd->bqhd", weights_low, value_rows)
    attended = attended.reshape(row_count, part_width).astype(jnp.bfloat16)
    kept_out = select_rows(mult("tc,cj->tj", attended, a_out), onehot, image_len)
    out_terms = mult("tc,cd->td", attended, wide_out) + mult("tj,jd->td", kept_out, b_out)
    hidden = inputs + sum_partials(out_terms) + own_part(out_bias, 0)
    normal_two, inverse_two = norm_split(hidden, feature_width)
    normed_part_two = (normal_two * own_part(ln2_gain, 0) + own_part(ln2_bias, 0)).astype(
        jnp.bfloat16
    )
    normed_two = gather_features(normed_part_two)
    kept_up = select_rows(mult("td,dj->tj", normed_two, a_up), onehot, image_len)
    pre_up = mult("td,df->tf", normed_two, wide_up) + mult("tj,jf->tf", kept_up, b_up) + up_bias
    logistic = jax.nn.sigmoid(GELU_SCALE * pre_up)
    activated = (pre_up * logistic).astype(jnp.bfloat16)
    kept_down = select_rows(mult("tf,fj->tj", activated, a_down), onehot, image_len)
    down_terms = mult("tf,fd->td", activated, wide_down) + mult("tj,jd->td", kept_down, b_down)
    layer_out = (hidden + sum_partials(down_terms) + own_part(down_bias, 0)).astype(jnp.bfloat16)
    wide_qkv, wide_out, wide_up, wide_down = (
        lax.all_gather(w_qkv, "row", axis=1, tiled=True),
        lax.all_gather(w_out, "row", axis=1, tiled=True),
        lax.all_gather(w_up, "row", axis=0, tiled=True),
        lax.all_gather(w_down, "row", axis=1, tiled=True),
    )
    grad_layer = cotangent.astype(jnp.float32)
    grad_full = gather_features(cotangent)
    d_low_down = select_rows(mult("td,jd->tj", grad_full, b_down), onehot, image_len)
    d_activated = mult("td,fd->tf", grad_full, wide_down) + mult("tj,fj->tf", d_low_down, a_down)
    grad_b_down = mult("tj,td->jd", kept_down, grad_full)
    grad_a_down = mult("tf,tj->fj", activated, d_low_down)
    d_pre_up = (
        d_activated * (logistic + GELU_SCALE * pre_up * logistic * (1.0 - logistic))
    ).astype(jnp.bfloat16)
    d_low_up = select_rows(mult("tf,jf->tj", d_pre_up, b_up), onehot, image_len)
    grad_b_up = mult("tj,tf->jf", kept_up, d_pre_up)
    grad_a_up = mult("td,tj->dj", normed_two, d_low_up)
    normed_two_terms = mult("tf,df->td", d_pre_up, wide_up) + mult("tj,dj->td", d_low_up, a_up)
    d_normed_two = sum_partials(normed_two_terms)
    grad_hidden = grad_layer + norm_back(
        d_normed_two, normal_two, inverse_two, own_part(ln2_gain, 0), feature_width
    )
    hidden_full_grad = gather_features(grad_hidden.astype(jnp.bfloat16))
    d_low_out = select_rows(mult("td,jd->tj", hidden_full_grad, b_out), onehot, image_len)
    d_attended = mult("td,cd->tc", hidden_full_grad, wide_out) + mult("tj,cj->tc", d_low_out, a_out)
    grad_b_out = mult("tj,td->jd", kept_out, hidden_full_grad)
    grad_a_out = mult("tc,tj->cj", attended, d_low_out)
    d_heads = d_attended.astype(jnp.bfloat16).reshape(image_count, image_len, head_count, HD)
    scores_again = mult("bqhd,bkhd->bhqk", queries, key_rows) * scale
    weights_again = jnp.exp(scores_again - log_total)
    weights_again_low = weights_again.astype(jnp.bfloat16)
    d_weights = mult("bqhd,bkhd->bhqk", d_heads, value_rows)
    d_values = mult("bhqk,bqhd->bkhd", weights_again_low, d_heads)
    d_scores = weights_again * (
        d_weights - jnp.sum(weights_again * d_weights, axis=-1, keepdims=True)
    )
    d_scores = d_scores.astype(jnp.bfloat16)
    d_queries = scale * mult("bhqk,bkhd->bqhd", d_scores, key_rows)
    d_keys = scale * mult("bhqk,bqhd->bkhd", d_scores, queries)
    d_qkv = (
        jnp.stack([d_queries, d_keys, d_values])
        .reshape(3, row_count, part_width)
        .astype(jnp.bfloat16)
    )
    d_low_qkv = mult("kte,kje->tkj", d_qkv, b_qkv)
    d_low_qkv = select_rows(d_low_qkv.reshape(row_count, 3 * stack_width), onehot, image_len)
    grad_b_qkv = mult("tkj,kte->kje", kept_qkv.reshape(row_count, 3, stack_width), d_qkv)
    grad_a_qkv = mult("td,tj->dj", normed_one, d_low_qkv)
    normed_one_terms = mult("kte,kde->td", d_qkv, wide_qkv) + mult("tj,dj->td", d_low_qkv, a_qkv)
    d_normed_one = sum_partials(normed_one_terms)
    tokens_grad = grad_hidden + norm_back(
        d_normed_one, normal_one, inverse_one, own_part(ln1_gain, 0), feature_width
    )
    grad_a_qkv, grad_b_out, grad_a_up, grad_b_down = lax.psum(
        (grad_a_qkv, grad_b_out, grad_a_up, grad_b_down), ("row", "col")
    )
    grad_b_qkv, grad_a_out, grad_b_up, grad_a_down = (
        lax.psum(grad_b_qkv.astype(jnp.bfloat16), "row").astype(jnp.float32),
        lax.psum(grad_a_out.astype(jnp.bfloat16), "row").astype(jnp.float32),
        lax.psum(grad_b_up.astype(jnp.bfloat16), "row").astype(jnp.float32),
        lax.psum(grad_a_down.astype(jnp.bfloat16), "row").astype(jnp.float32),
    )
    return (
        layer_out,
        tokens_grad,
        grad_a_qkv,
        grad_b_qkv,
        grad_a_out,
        grad_b_out,
        grad_a_up,
        grad_b_up,
        grad_a_down,
        grad_b_down,
    )


def solution(mesh):
    placed = (
        P("row", "col"),
        P("row", "col"),
        P(),
        P(),
        P(),
        P(),
        P(None, "row", "col"),
        P(None, "col"),
        P("col", "row"),
        P(),
        P("row", "col"),
        P("col"),
        P("col", "row"),
        P(),
        P("row"),
        P(),
        P(None, None, "col"),
        P("col", None),
        P(),
        P(),
        P(None, "col"),
        P("col", None),
        P(),
    )
    return jax.shard_map(
        on_device,
        mesh=mesh,
        in_specs=placed,
        out_specs=(
            P("row", "col"),
            P("row", "col"),
            P(),
            P(None, None, "col"),
            P("col", None),
            P(),
            P(),
            P(None, "col"),
            P("col", None),
            P(),
        ),
        check_vma=False,
    )
```

profile of v0, /device:TPU:0, one launch (start us, length us, event | category | flops | bytes accessed | tf_op | source)
XLA Modules:
  0.0 1170.5 jit_solution(5493868840499844327)
XLA Ops:
  10.9 9.6 all-reduce.4
  28.5 45.2 %all-gather.9.cloned.1.call-done = bf16[1731,1024]{1,0:T(8,128)(2,1)} async-done(((bf16[1731,512]{1,0:T(8,128)(2,1)}), bf16[1731,1024]{1,0:T(8,128)(2,1)}) %all-gather.9.cloned.1.call-update) | async-done | bytes 3545104 | tf_op jit(solution)/shard_map/all_gather | solution.py:19
  73.7 5.9 fusion.21
  81.5 39.7 %all-gather.11.cloned.1.call-done = bf16[3,1024,512]{2,1,0:T(8,128)(2,1)} async-done(((bf16[3,64,512]{2,1,0:T(8,128)(2,1)}), bf16[3,1024,512]{2,1,0:T(8,128)(2,1)}) %all-gather.11.cloned.1.call-update) | async-done | bytes 3145744 | tf_op jit(solution)/shard_map/all_gather | solution.py:93
  121.1 8.8 fusion.17
  133.8 5.6 reshape.156
  139.3 5.5 copy.55
  144.9 5.6 reshape.155
  150.4 5.8 copy.54
  156.2 3.6 reshape.154
  159.8 5.6 copy.56
  165.3 19.7 %multiply_reduce_fusion.1 = (f32[3,8,577]{2,1,0:T(8,128)S(1)}, f32[3,8,577,577]{2,3,1,0:T(8,128)}) fusion(bf16[3,577,8,64]{1,3,2,0:T(8,128)(2,1)} %copy.54, bf16[3,577,8,64]{1,3,2,0:T(8,128)(2,1)} %copy.55), kind=kOutput, calls=%fused_computation.4 | convolution fusion | flops 1038724608 | bytes 35561664 | tf_op jit(solution)/shard_map/bqhd,bkhd->bhqk/dot_general | solution.py:50
  185.1 15.2 %exponential_reduce_fusion = f32[3,8,577]{2,1,0:T(8,128)S(1)} fusion(f32[3,8,577,577]{2,3,1,0:T(8,128)} %get-tuple-element.47, f32[3,8,577]{2,1,0:T(8,128)S(1)} %get-tuple-element.46), kind=kLoop, calls=%fused_computation.3 | loop fusion | flops 23957040 | bytes 32071968 | tf_op jit(solution)/shard_map/reduce_sum | solution.py:111
  200.4 16.4 %fusion.33 = bf16[3,8,64,577]{3,2,1,0:T(8,128)(2,1)} fusion(bf16[3,577,8,64]{1,3,2,0:T(8,128)(2,1)S(1)} %copy-done.8, f32[3,8,577,577]{2,3,1,0:T(8,128)} %get-tuple-element.47, f32[3,8,577]{2,1,0:T(8,128)S(1)} %log_add_fusion), kind=kOutput, calls=%fused_computation.71 | convolution fusion | flops 1047615040 | bytes 35561664 | tf_op jit(solution)/shard_map/bhqk,bkhd->bqhd/dot_general | solution.py:50
  219.2 4.9 copy.58
  224.1 6.0 convert_element_type.140
  230.1 4.0 fusion.46
  238.6 45.4 %reduce-scatter.5.cloned.1.call-done = bf16[1731,512]{1,0:T(8,128)(2,1)} async-done(((bf16[1731,1024]{1,0:T(8,128)(2,1)}), bf16[1731,512]{1,0:T(8,128)(2,1)}) %reduce-scatter.5.cloned.1.call-update) | async-done | bytes 1772560 | tf_op jit(solution)/shard_map/reduce_scatter | solution.py:23
  286.4 6.9 all-reduce.3
  293.3 3.5 add_convert_fusion.5
  299.8 35.2 %all-gather.21.cloned.1.call-done = bf16[1731,1024]{1,0:T(8,128)(2,1)} async-done(((bf16[1731,512]{1,0:T(8,128)(2,1)}), bf16[1731,1024]{1,0:T(8,128)(2,1)}) %all-gather.21.cloned.1.call-update) | async-done | bytes 3545104 | tf_op jit(solution)/shard_map/all_gather | solution.py:19
  335.0 4.0 fusion.27
  338.9 49.0 %all-gather.19.cloned.1.call-done = bf16[2048,1024]{0,1:T(8,128)(2,1)} async-done(((bf16[2048,64]{0,1:T(8,128)(2,1)}), bf16[2048,1024]{0,1:T(8,128)(2,1)}) %all-gather.19.cloned.1.call-update) | async-done | bytes 4194320 | tf_op jit(solution)/shard_map/all_gather | solution.py:96
  388.0 13.5 %fusion.49 = f32[1731,2048]{1,0:T(8,128)} fusion(bf16[1731,1024]{1,0:T(8,128)(2,1)} %all-gather.21.cloned.1.call-done, bf16[2048,1024]{0,1:T(8,128)(2,1)} %all-gather.19.cloned.1.call-done), kind=kOutput, calls=%fused_computation.102 | convolution fusion | flops 7260340224 | bytes 21919744 | tf_op jit(solution)/shard_map/td,fd->tf/dot_general | solution.py:50
  401.5 36.8 %all-gather.15.cloned.1.call-done = bf16[1731,1024]{1,0:T(8,128)(2,1)} async-done(((bf16[1731,512]{1,0:T(8,128)(2,1)}), bf16[1731,1024]{1,0:T(8,128)(2,1)}) %all-gather.15.cloned.1.call-update) | async-done | bytes 3545104 | tf_op jit(solution)/shard_map/all_gather | solution.py:19
  438.3 3.9 fusion.26
  442.2 49.1 %all-gather.17.cloned.1.call-done = bf16[1024,2048]{1,0:T(8,128)(2,1)} async-done(((bf16[64,2048]{1,0:T(8,128)(2,1)}), bf16[1024,2048]{1,0:T(8,128)(2,1)}) %all-gather.17.cloned.1.call-update) | async-done | bytes 4194320 | tf_op jit(solution)/shard_map/all_gather | solution.py:95
  491.2 13.4 %fusion.47 = f32[1731,2048]{1,0:T(8,128)} fusion(bf16[1731,1024]{1,0:T(8,128)(2,1)} %all-gather.15.cloned.1.call-done, bf16[1024,2048]{1,0:T(8,128)(2,1)} %all-gather.17.cloned.1.call-done), kind=kOutput, calls=%fused_computation.100 | convolution fusion | flops 7260340224 | bytes 21919744 | tf_op jit(solution)/shard_map/td,df->tf/dot_general | solution.py:50
  504.7 12.5 %multiply_convert_fusion.2 = (bf16[1731,2048]{1,0:T(8,128)(2,1)}, f32[1731,2048]{1,0:T(8,128)}) fusion(f32[2048]{0:T(1024)S(1)} %copy-done.56, f32[1731,2048]{1,0:T(8,128)} %fusion.47, bf16[1731,128]{1,0:T(8,128)(2,1)S(1)} %copy-done.22, bf16[128,2048]{1,0:T(8,128)(2,1)S(1)} %copy-done.34), kind=kOutput, calls=%fused_computation.7 | convolution fusion | flops 935903232 | bytes 36426496 | tf_op jit(solution)/shard_map/tj,jf->tf/dot_general | solution.py:50
  517.1 12.4 %multiply_convert_fusion.1 = bf16[1731,2048]{1,0:T(8,128)(2,1)S(1)} fusion(f32[1731,2048]{1,0:T(8,128)} %fusion.49, f32[1731,2048]{1,0:T(8,128)} %get-tuple-element.49, bf16[1731,128]{1,0:T(8,128)(2,1)S(1)} %copy-done.32, bf16[2048,128]{1,0:T(8,128)(2,1)S(1)} %copy-done.35), kind=kOutput, calls=%fused_computation.6 | convolution fusion | flops 946538496 | bytes 36418304 | tf_op jit(solution)/shard_map/tj,fj->tf/dot_general | solution.py:50
  534.3 7.9 fusion.50
  545.7 5.3 fusion.29
  551.0 10.1 fusion.48
  564.7 27.0 %reduce-scatter.9.cloned.1.call-done = bf16[1731,512]{1,0:T(8,128)(2,1)} async-done(((bf16[1731,1024]{1,0:T(8,128)(2,1)}), bf16[1731,512]{1,0:T(8,128)(2,1)}) %reduce-scatter.9.cloned.1.call-update) | async-done | bytes 1772560 | tf_op jit(solution)/shard_map/reduce_scatter | solution.py:23
  591.8 3.5 fusion.20
  595.3 6.9 all-reduce.2
  602.2 39.6 %reduce-scatter.7.cloned.1.call-done = bf16[1731,512]{1,0:T(8,128)(2,1)} async-done(((bf16[1731,1024]{1,0:T(8,128)(2,1)}), bf16[1731,512]{1,0:T(8,128)(2,1)}) %reduce-scatter.7.cloned.1.call-update) | async-done | bytes 1772560 | tf_op jit(solution)/shard_map/reduce_scatter | solution.py:23
  641.8 6.3 fusion.43
  648.4 5.3 convolution_convert_fusion.1
  653.7 7.0 convolution_convert_fusion
  660.7 37.2 %all-gather.23.cloned.1.call-done = bf16[1731,1024]{1,0:T(8,128)(2,1)} async-done(((bf16[1731,512]{1,0:T(8,128)(2,1)}), bf16[1731,1024]{1,0:T(8,128)(2,1)}) %all-gather.23.cloned.1.call-update) | async-done | bytes 3545104 | tf_op jit(solution)/shard_map/all_gather | solution.py:19
  706.5 5.8 reshape.157
  712.3 5.5 copy.61
  717.8 16.3 %convert_bitcast_fusion = bf16[3,577,8,64]{1,3,2,0:T(8,128)(2,1)} fusion(bf16[3,577,8,64]{1,3,2,0:T(8,128)(2,1)} %copy.61, f32[3,8,577,577]{2,3,1,0:T(8,128)} %get-tuple-element.47, f32[3,8,577]{2,1,0:T(8,128)S(1)} %copy-done.28), kind=kOutput, calls=%fused_computation.70 | convolution fusion | flops 1047615040 | bytes 35561664 | tf_op jit(solution)/shard_map/bhqk,bqhd->bkhd/dot_general | solution.py:50
  734.1 27.9 %multiply_reduce_fusion = (f32[3,8,577]{2,1,0:T(8,128)S(1)}, f32[3,8,577,577]{2,3,1,0:T(8,128)}) fusion(f32[3,8,577,577]{2,3,1,0:T(8,128)} %get-tuple-element.47, f32[3,8,577]{2,1,0:T(8,128)S(1)} %copy-done.28, bf16[3,577,8,64]{1,3,2,0:T(8,128)(2,1)} %copy.61, bf16[3,577,8,64]{1,3,2,0:T(8,128)(2,1)} %copy.56), kind=kOutput, calls=%fused_computation.1 | convolution fusion | flops 1054705216 | bytes 67578240 | tf_op jit(solution)/shard_map/bqhd,bkhd->bhqk/dot_general | solution.py:50
  762.0 29.7 %multiply_convert_fusion = bf16[3,8,577,577]{2,3,1,0:T(8,128)(2,1)} fusion(f32[3,8,577,577]{2,3,1,0:T(8,128)} %get-tuple-element.51, f32[3,8,577,577]{2,3,1,0:T(8,128)} %get-tuple-element.47, f32[3,8,577]{2,1,0:T(8,128)S(1)} %get-tuple-element.50, f32[3,8,577]{2,1,0:T(8,128)S(1)} %copy-done.28), kind=kLoop, calls=%fused_computation | loop fusion | flops 39951480 | bytes 80013744 | tf_op jit(solution)/shard_map/convert_element_type | solution.py:167
  791.8 10.7 fusion.32
  802.5 10.7 fusion.31
  813.2 5.5 copy.87
  818.7 5.8 reshape.153
  824.5 5.5 copy.85
  830.1 5.8 reshape.151
  835.9 5.5 copy.86
  841.4 5.8 reshape.152
  854.0 5.6 convolution_bitcast_fusion
  859.6 3.4 copy.75
  866.4 9.1 fusion.52
  877.0 3.9 fusion.3
  882.0 4.2 fusion.55
  893.0 69.6 %all-reduce.11.cloned.1.call-done = (bf16[3,128,512]{2,1,0:T(8,128)(2,1)}, bf16[512,128]{1,0:T(8,128)(2,1)}, bf16[128,2048]{1,0:T(8,128)(2,1)}, bf16[2048,128]{1,0:T(8,128)(2,1)}) async-done(((bf16[3,128,512]{2,1,0:T(8,128)(2,1)}, bf16[512,128]{1,0:T(8,128)(2,1)}, bf16[128,2048]{1,0:T(8,128)(2,1)}, bf16[2048,128]{1,0:T(8,128)(2,1)}), (bf16[3,128,512]{2,1,0:T(8,128)(2,1)}, bf16[512,128]{1,0:T(8,128)(2,1)}, ...) | async-done | bytes 1572880 | tf_op jit(solution)/shard_map/psum | solution.py:188
  970.4 41.3 %reduce-scatter.11.cloned.1.call-done = bf16[1731,512]{1,0:T(8,128)(2,1)} async-done(((bf16[1731,1024]{1,0:T(8,128)(2,1)}), bf16[1731,512]{1,0:T(8,128)(2,1)}) %reduce-scatter.11.cloned.1.call-update) | async-done | bytes 1772560 | tf_op jit(solution)/shard_map/reduce_scatter | solution.py:23
  1014.8 6.9 all-reduce.1
  1021.7 4.6 fusion.14
  1026.3 130.9 %all-reduce.9.cloned.1.call-done = (f32[1024,384]{1,0:T(8,128)}, f32[128,1024]{1,0:T(8,128)}, f32[1024,128]{1,0:T(8,128)}, f32[128,1024]{1,0:T(8,128)}) async-done(((f32[1024,384]{1,0:T(8,128)}, f32[128,1024]{1,0:T(8,128)}, f32[1024,128]{1,0:T(8,128)}, f32[128,1024]{1,0:T(8,128)}), (f32[1024,384]{1,0:T(8,128)}, f32[128,1024]{1,0:T(8,128)}, f32[1024,128]{1,0:T(8,128)}, ...) | async-done | bytes 3145744 | tf_op jit(solution)/shard_map/psum | solution.py:184
  (198 shorter events, 86.5 us)
Async XLA Ops:
  7.2 66.5 %copy-start = (bf16[1024,384]{1,0:T(8,128)(2,1)S(1)}, bf16[1024,384]{1,0:T(8,128)(2,1)}, u32[]{:S(2)}) copy-start(bf16[1024,384]{1,0:T(8,128)(2,1)} %param.38) | copy-start | bytes 2359300
  7.2 66.5 %all-gather.9.cloned.1.call-start = ((), (), s32[]{:S(2)}) async-start(), calls=%async_computation.4 | async-start | bytes 5332992 | tf_op jit(solution)/shard_map/all_gather | solution.py:19
  8.1 15.7 %copy-start.44 = (f32[512]{0:T(512)}, f32[512]{0:T(512)S(1)}, u32[]{:S(2)}) copy-start(f32[512]{0:T(512)S(1)} %dynamic_slice.20) | copy-start | bytes 6148
  8.8 16.5 %copy-start.46 = (f32[2,512]{1,0:T(2,128)S(1)}, f32[2,512]{1,0:T(2,128)}, u32[]{:S(2)}) copy-start(f32[2,512]{1,0:T(2,128)} %param.30) | copy-start | bytes 12292
  8.8 16.5 %copy-start.51 = (s32[3]{0:T(128)S(1)}, s32[3]{0:T(128)}, u32[]{:S(2)}) copy-start(s32[3]{0:T(128)} %param.37) | copy-start | bytes 40
  20.6 5.3 copy-start.40
  20.6 5.3 copy-start.42
  23.8 97.4 %all-gather.11.cloned.1.call-start = ((), (), s32[]{:S(2)}) async-start(), calls=%async_computation.5 | async-start | bytes 3342336 | tf_op jit(solution)/shard_map/all_gather | solution.py:93
  24.5 205.6 %all-gather.13.cloned.1.call-start = ((), (), s32[]{:S(2)}) async-start(), calls=%async_computation.6 | async-start | bytes 1114112 | tf_op jit(solution)/shard_map/all_gather | solution.py:94
  25.3 258.7 %reduce-scatter.5.cloned.1.call-start = ((), (), s32[]{:S(2)}) async-start(), calls=%async_computation.7 | async-start | bytes 5332992 | tf_op jit(solution)/shard_map/reduce_scatter | solution.py:23
  81.4 48.5 %copy-start.9 = (bf16[1731,384]{0,1:T(8,128)(2,1)}, bf16[1731,384]{0,1:T(8,128)(2,1)S(1)}, u32[]{:S(2)}) copy-start(bf16[1731,384]{0,1:T(8,128)(2,1)S(1)} %copy.49) | copy-start | bytes 3988228
  81.5 48.5 %copy-start.25 = (bf16[3,128,512]{2,1,0:T(8,128)(2,1)S(1)}, bf16[3,128,512]{2,1,0:T(8,128)(2,1)}, u32[]{:S(2)}) copy-start(bf16[3,128,512]{2,1,0:T(8,128)(2,1)} %param.39) | copy-start | bytes 1179652
  185.1 15.3 %copy-start.8 = (bf16[3,577,8,64]{1,3,2,0:T(8,128)(2,1)S(1)}, bf16[3,577,8,64]{1,3,2,0:T(8,128)(2,1)}, u32[]{:S(2)}) copy-start(bf16[3,577,8,64]{1,3,2,0:T(8,128)(2,1)} %copy.56) | copy-start | bytes 5317636
  200.3 16.5 %copy-start.27 = (f32[3,8,577]{2,1,0:T(8,128)}, f32[3,8,577]{2,1,0:T(8,128)S(1)}, u32[]{:S(2)}) copy-start(f32[3,8,577]{2,1,0:T(8,128)S(1)} %log_add_fusion) | copy-start | bytes 166180
  200.3 16.5 %copy-start.36 = (bf16[512,128]{1,0:T(8,128)(2,1)S(1)}, bf16[512,128]{1,0:T(8,128)(2,1)}, u32[]{:S(2)}) copy-start(bf16[512,128]{1,0:T(8,128)(2,1)} %param.40) | copy-start | bytes 393220
  219.2 15.0 %copy-start.23 = (bf16[1731,128]{1,0:T(8,128)(2,1)}, bf16[1731,128]{1,0:T(8,128)(2,1)S(1)}, u32[]{:S(2)}) copy-start(bf16[1731,128]{1,0:T(8,128)(2,1)S(1)} %convert_element_type.143) | copy-start | bytes 1329412
  230.1 4.1 copy-start.31
  237.1 46.9 %copy-start.1 = (bf16[1731,512]{1,0:T(8,128)(2,1)S(1)}, bf16[1731,512]{1,0:T(8,128)(2,1)}, u32[]{:S(2)}) copy-start(bf16[1731,512]{1,0:T(8,128)(2,1)} %param.23) | copy-start | bytes 5317636
  237.1 97.9 %all-gather.21.cloned.1.call-start = ((), (), s32[]{:S(2)}) async-start(), calls=%async_computation.12 | async-start | bytes 5332992 | tf_op jit(solution)/shard_map/all_gather | solution.py:19
  237.7 150.3 %all-gather.19.cloned.1.call-start = ((), (), s32[]{:S(2)}) async-start(), calls=%async_computation.10 | async-start | bytes 4456448 | tf_op jit(solution)/shard_map/all_gather | solution.py:96
  238.3 200.0 %all-gather.15.cloned.1.call-start = ((), (), s32[]{:S(2)}) async-start(), calls=%async_computation.8 | async-start | bytes 5332992 | tf_op jit(solution)/shard_map/all_gather | solution.py:19
  296.8 194.4 %all-gather.17.cloned.1.call-start = ((), (), s32[]{:S(2)}) async-start(), calls=%async_computation.9 | async-start | bytes 4456448 | tf_op jit(solution)/shard_map/all_gather | solution.py:95
  297.6 294.2 %reduce-scatter.9.cloned.1.call-start = ((), (), s32[]{:S(2)}) async-start(), calls=%async_computation.13 | async-start | bytes 5332992 | tf_op jit(solution)/shard_map/reduce_scatter | solution.py:23
  442.2 62.5 %copy-start.56 = (f32[2048]{0:T(1024)S(1)}, f32[2048]{0:T(1024)}, u32[]{:S(2)}) copy-start(f32[2048]{0:T(1024)} %param.34) | copy-start | bytes 24580
  491.2 13.4 %copy-start.22 = (bf16[1731,128]{1,0:T(8,128)(2,1)S(1)}, bf16[1731,128]{1,0:T(8,128)(2,1)}, u32[]{:S(2)}) copy-start(bf16[1731,128]{1,0:T(8,128)(2,1)} %fusion.26) | copy-start | bytes 1329412
  491.2 13.4 %copy-start.34 = (bf16[128,2048]{1,0:T(8,128)(2,1)S(1)}, bf16[128,2048]{1,0:T(8,128)(2,1)}, u32[]{:S(2)}) copy-start(bf16[128,2048]{1,0:T(8,128)(2,1)} %param.43) | copy-start | bytes 1572868
  504.6 12.5 %copy-start.32 = (bf16[1731,128]{1,0:T(8,128)(2,1)S(1)}, bf16[1731,128]{1,0:T(8,128)(2,1)}, u32[]{:S(2)}) copy-start(bf16[1731,128]{1,0:T(8,128)(2,1)} %fusion.27) | copy-start | bytes 1329412
  504.7 12.5 %copy-start.35 = (bf16[2048,128]{1,0:T(8,128)(2,1)S(1)}, bf16[2048,128]{1,0:T(8,128)(2,1)}, u32[]{:S(2)}) copy-start(bf16[2048,128]{1,0:T(8,128)(2,1)} %param.44) | copy-start | bytes 1572868
  529.6 3.6 copy-start.2
  529.6 4.8 copy-start.53
  534.3 7.9 copy-start.18
  534.3 7.9 copy-start.29
  545.2 96.6 %reduce-scatter.7.cloned.1.call-start = ((), (), s32[]{:S(2)}) async-start(), calls=%async_computation.11 | async-start | bytes 5332992 | tf_op jit(solution)/shard_map/reduce_scatter | solution.py:23
  545.7 5.3 copy-start.52
  551.0 10.1 copy-start.20
  551.0 10.1 copy-start.30
  564.0 133.9 %all-gather.23.cloned.1.call-start = ((), (), s32[]{:S(2)}) async-start(), calls=%async_computation.14 | async-start | bytes 5332992 | tf_op jit(solution)/shard_map/all_gather | solution.py:19
  648.2 314.4 %all-reduce.11.cloned.1.call-start = ((), (), s32[]{:S(2)}) async-start(), calls=%async_computation.17 | async-start | bytes 3145728 | tf_op jit(solution)/shard_map/psum | solution.py:188
  648.4 5.3 copy-start.33
  697.9 3.3 copy-start.13
  697.9 4.6 copy-start.5
  697.9 4.6 copy-start.55
  702.5 2.1 copy-start.37
  712.3 5.5 copy-start.28
  791.8 10.7 copy-start.7
  847.3 2.0 copy-start.15
  847.3 2.5 copy-start.14
  849.3 3.0 copy-start.10
  849.9 2.4 copy-start.3
  866.3 145.4 %reduce-scatter.11.cloned.1.call-start = ((), (), s32[]{:S(2)}) async-start(), calls=%async_computation.15 | async-start | bytes 5332992 | tf_op jit(solution)/shard_map/reduce_scatter | solution.py:23
  866.3 9.2 copy-start.11
  866.4 9.2 copy-start.12
  881.0 5.3 copy-start.21
  881.0 276.2 %all-reduce.9.cloned.1.call-start = ((), (), s32[]{:S(2)}) async-start(), calls=%async_computation.16 | async-start | bytes 6291456 | tf_op jit(solution)/shard_map/psum | solution.py:184
  882.0 4.3 copy-start.4
  882.0 6.0 copy-start.6
  882.0 6.0 copy-start.24
  886.2 3.5 copy-start.17
  886.2 3.5 copy-start.54
  893.0 118.7 %copy-start.41 = (f32[1731]{0:T(1024)S(1)}, f32[1731]{0:T(1024)}, u32[]{:S(2)}) copy-start(f32[1731]{0:T(1024)} %copy-done.40) | copy-start | bytes 20776
  893.0 118.7 %copy-start.43 = (f32[1731]{0:T(1024)S(1)}, f32[1731]{0:T(1024)}, u32[]{:S(2)}) copy-start(f32[1731]{0:T(1024)} %copy-done.42) | copy-start | bytes 20776
  893.0 118.7 %copy-start.45 = (f32[512]{0:T(512)S(1)}, f32[512]{0:T(512)}, u32[]{:S(2)}) copy-start(f32[512]{0:T(512)} %copy-done.44) | copy-start | bytes 6148
  1157.2 4.6 copy-start.39
  1157.2 5.4 copy-start.38
  (7 other events, 8.4 us)
Sparse Core Ops, SparseCore 0:
  23.9 49.7 all-gather.8
  75.9 45.1 all-gather.10
  123.3 36.7 all-gather.12
  237.2 46.6 reduce-scatter.4
  285.4 49.5 all-gather.20
  337.2 50.7 all-gather.18
  390.2 48.0 all-gather.14
  440.6 50.5 all-gather.16
  545.4 46.3 reduce-scatter.8
  593.8 47.9 reduce-scatter.6
  648.3 49.5 all-gather.22
  866.4 96.1 all-reduce.10
  964.9 46.6 reduce-scatter.10
  1018.5 138.6 all-reduce.8
where the time goes:
time: 1180 us; the launch traced here: 1170 us
  waiting for transfers between devices  649 us (55%)
  matrix products  270 us (23%)
  local copies, waits for them, and re-layouts  122 us (10%)
  other arithmetic  82.1 us (7%)
  blocking collectives  30.3 us (3%)
  between operations  15.1 us (1%)
    dot_general x38, matrix products, mult(): return jnp.einsum(form, first, second, preferred_element_type=jnp.float32)  270 us
    all_gather x4, waiting for transfers between devices, gather_features(): return lax.all_gather(values, 'col', axis=1, tiled=True)  154 us
    reduce_scatter x4, waiting for transfers between devices, sum_partials(): lax.psum_scatter(terms.astype(jnp.bfloat16), 'col', scatter_dimension=1,...  153 us
    psum x1, waiting for transfers between devices, on_device(): lax.psum((grad_a_qkv, grad_b_out, grad_a_up, grad_b_down), ('row', 'col'))  131 us
    psum x1, waiting for transfers between devices, on_device(): lax.psum(grad_b_qkv.astype(jnp.bfloat16), 'row').astype(jnp.float32)  69.6 us
    all_gather x1, waiting for transfers between devices, on_device(): lax.all_gather(w_up, 'row', axis=0, tiled=True)  49.1 us
    all_gather x1, waiting for transfers between devices, on_device(): lax.all_gather(w_down, 'row', axis=1, tiled=True)  49 us
    all_gather x1, waiting for transfers between devices, on_device(): lax.all_gather(w_qkv, 'row', axis=1, tiled=True)  39.7 us
  transfers between devices with their start and end apart: 14, of which 13 were waited for; matrix products, arithmetic and copies ran while one was open for 19% of the time, Pallas kernels for 0%

commit v1 on v0

--- a/solution.py
+++ b/solution.py
@@ -1,6 +1,10 @@
+import functools
+
 import jax
 import jax.numpy as jnp
 from jax import lax
+from jax.experimental import pallas as pl
+from jax.experimental.pallas import tpu as pltpu
 from jax.sharding import PartitionSpec as P
 
 HD = 64
@@ -204,6 +208,938 @@
     )
 
 
+NT = (((1,), (1,)), ((), ()))
+NN = (((1,), (0,)), ((), ()))
+F32 = jnp.float32
+BF16 = jnp.bfloat16
+VMEM_LIMIT = 60 * 1024 * 1024
+SPOT = pl.BlockSpec(memory_space=pltpu.SMEM)
+
+
+def dot(first, second, dims=NN):
+    return lax.dot_general(first, second, dims, preferred_element_type=F32)
+
+
+def dot_rows(first, second):
+    return dot(first.T, second)
+
+
+def call(body, grid, in_specs, out_specs, out_shape, scratch=()):
+    return pl.pallas_call(
+        body,
+        grid=grid,
+        in_specs=in_specs,
+        out_specs=out_specs,
+        out_shape=out_shape,
+        scratch_shapes=list(scratch),
+        compiler_params=pltpu.CompilerParams(
+            dimension_semantics=("arbitrary",) * len(grid), vmem_limit_bytes=VMEM_LIMIT
+        ),
+    )
+
+
+def fixed(shape):
+    zeros = (0,) * len(shape)
+    return pl.BlockSpec(shape, lambda *_: zeros, pipeline_mode=pl.Buffered(1))
+
+
+def struct(shape, kind):
+    return jax.ShapeDtypeStruct(shape, kind)
+
+
+def norm_of(values):
+    centred = values - jnp.mean(values, axis=1, keepdims=True)
+    inverse = lax.rsqrt(jnp.mean(centred * centred, axis=1, keepdims=True) + EPS)
+    return centred * inverse, inverse
+
+
+def norm_pull(grad, normal, inverse, gain):
+    scaled = grad * gain
+    return inverse * (
+        scaled
+        - jnp.mean(scaled, axis=1, keepdims=True)
+        - normal * jnp.mean(scaled * normal, axis=1, keepdims=True)
+    )
+
+
+def settle(place, pieces, side_first, store):
+    depth = pieces[0].shape[0]
+    n_far = depth // 2
+    for group, piece in enumerate(pieces):
+        for index in range(depth):
+            other, outer, inner, back = (
+                group // 2, group % 2, index // n_far, index % n_far
+            )
+            x_off, y_off = (outer, inner) if side_first else (inner, outer)
+            far = lax.rem(place[0] + (n_far - back), n_far)
+            x = place[1] if x_off == 0 else 1 - place[1]
+            core = place[2] if other == 0 else 1 - place[2]
+            y = place[3] if y_off == 0 else 1 - place[3]
+            store(far * 4 + x * 2 + core, y, piece[index])
+
+
+def settle_qkv(place, pieces0, pieces1, w_ref):
+    half = pieces1[0].shape[2]
+
+    def lanes(y):
+        return pl.ds(pl.multiple_of(y * half, half), half)
+
+    def first(row, y, block):
+        w_ref[0, row, :, lanes(y)] = block[:, :half]
+        w_ref[1, row, :, lanes(y)] = block[:, half:]
+
+    def last(row, y, block):
+        w_ref[2, row, :, lanes(y)] = block
+
+    settle(place, pieces0, False, first)
+    settle(place, pieces1, True, last)
+
+
+def settle_out(place, pieces1, w_ref):
+    half = pieces1[0].shape[2]
+
+    def store(row, y, block):
+        w_ref[row, :, pl.ds(pl.multiple_of(y * half, half), half)] = block
+
+    settle(place, pieces1, True, store)
+
+
+def chosen(index, first, second):
+    return jnp.where(index == 0, first, second)
+
+
+def both_halves(place, own, near, far):
+    diagonal = place[2] == place[3]
+    mine = jnp.where(diagonal, own, near)
+    other = jnp.where(diagonal, near, far)
+    return chosen(place[3], mine, other), chosen(place[3], other, mine)
+
+
+def halves_out(place, values, rows, own_ref, near_ref, far_ref):
+    half = values.shape[1] // 2
+    left, right = values[:, :half], values[:, half:]
+    mine, other = chosen(place[3], left, right), chosen(place[3], right, left)
+    own_ref[rows, :] = mine
+    near_ref[rows, :] = jnp.where(place[2] == place[3], other, mine)
+    far_ref[rows, :] = other
+
+
+def spread_body(length, cut, own_rows, tb, place, t_ref, own_ref, near_ref, far_ref, wide_ref):
+    wide_ref[...] = t_ref[...].astype(F32)
+
+    def put(ref, start, shared, shared_count):
+        ref[:length, :] = wide_ref[start : start + length, :].astype(BF16)
+        ref[own_rows : own_rows + shared_count, :] = wide_ref[
+            shared : shared + shared_count, :
+        ].astype(BF16)
+
+    for ref, index in ((own_ref, place[2]), (near_ref, 1 - place[3]), (far_ref, 1 - place[2])):
+        ref[...] = jnp.zeros_like(ref)
+
+        @pl.when(index == 0)
+        def _():
+            put(ref, 0, length, cut)
+
+        @pl.when(index == 1)
+        def _():
+            put(ref, 2 * length, length + cut, length - cut)
+
+
+def join_body(length, cut, own_rows, place, own_ref, near_ref, far_ref, out_ref, wide_ref):
+    diagonal = place[2] == place[3]
+    mine = jnp.where(diagonal, own_ref[...], near_ref[...])
+    mate = jnp.where(diagonal, near_ref[...], far_ref[...])
+    first = chosen(place[2], mine, mate).astype(F32)
+    second = chosen(place[2], mate, mine).astype(F32)
+    wide_ref[:length, :] = first[:length]
+    wide_ref[length : length + cut, :] = first[own_rows : own_rows + cut]
+    wide_ref[length + cut : 2 * length, :] = second[own_rows : own_rows + length - cut]
+    wide_ref[2 * length :, :] = second[:length]
+    out_ref[...] = wide_ref[...].astype(out_ref.dtype)
+
+
+def qkv_body(
+    scale, place, own_ref, near_ref, far_ref, gain, bias, p0, p1, p2, p3, r0, r1, r2, r3, a_ref,
+    b_ref, qv_ref, sel_ref, x_ref, z_ref, u_ref, out_ref, keep_out, send_out, w_ref,
+):
+    width = x_ref.shape[1]
+    half = width // 2
+    stack = sel_ref.shape[1]
+
+    @pl.when(pl.program_id(0) == 0)
+    def _():
+        settle_qkv(place, (p0, p1, p2, p3), (r0, r1, r2, r3), w_ref)
+
+    left, right = both_halves(place, own_ref[...], near_ref[...], far_ref[...])
+    x = jnp.concatenate([left, right], axis=1)
+    x_ref[...] = x
+    normal, _ = norm_of(x.astype(F32))
+    z = (normal * gain[...] + bias[...]).astype(BF16)
+    z_ref[...] = z
+    low = dot(z, a_ref[...])
+    for k in range(3):
+        kept = (low[:, k * stack : (k + 1) * stack] * sel_ref[...]).astype(BF16)
+        u_ref[:, k * stack : (k + 1) * stack] = kept
+        w = w_ref[k].reshape(width, width)
+        parts = []
+        for y in range(2):
+            lanes = slice(y * half, (y + 1) * half)
+            acc = dot(z, w[:, lanes]) + dot(kept, b_ref[y, :, k * half : (k + 1) * half])
+            out = (acc + qv_ref[k, :, lanes]).astype(BF16)
+            if k == 0:
+                out = out * jnp.asarray(scale, BF16)
+            out_ref[k, :, lanes] = out
+            parts.append(out)
+        keep_out[k] = chosen(place[2], parts[0], parts[1])
+        send_out[k] = chosen(place[2], parts[1], parts[0])
+
+
+def attend_one(q, k, v, mask, p_ref):
+    lane = lax.broadcasted_iota(jnp.int32, q.shape, 1)
+    one, zero = jnp.ones_like(q), jnp.zeros_like(q)
+    parts = []
+    for head in range(2):
+        spare = HD if head == 0 else 0
+        here = lane < HD if head == 0 else lane >= HD
+        mine = jnp.where(here, q, jnp.where(lane == spare, one, zero))
+        s = dot(mine, jnp.where(lane == spare, mask, k), NT)
+        e = jnp.exp(s - jnp.max(s, axis=1, keepdims=True))
+        p = (e * (1.0 / jnp.sum(e, axis=1, keepdims=True))).astype(BF16)
+        p_ref[head] = p
+        parts.append(dot(p, v))
+    return jnp.where(lane < HD, parts[0], parts[1]).astype(BF16)
+
+
+def attend_body(q_ref, k_ref, v_ref, mask_ref, out_ref, p_ref):
+    out_ref[...] = attend_one(q_ref[0], k_ref[0], v_ref[0], mask_ref[...], p_ref)
+
+
+def attend_shared_body(mine_ref, mate_ref, mask_ref, keep_ref, send_ref, p_ref):
+    q, k, v = (jnp.concatenate([mine_ref[i], mate_ref[i]]) for i in range(3))
+    out = attend_one(q, k, v, mask_ref[...], p_ref)
+    keep_ref[...] = out[: keep_ref.shape[0]]
+    send_ref[...] = out[keep_ref.shape[0] :]
+
+
+def attend_back_one(scale, q, k, v, p_ref, att, do):
+    low_lanes = lax.broadcasted_iota(jnp.int32, q.shape, 1) < HD
+    zero = jnp.zeros_like(q)
+    product = att.astype(F32) * do.astype(F32)
+    dq = dk = dv = 0.0
+    for head in range(2):
+        here = low_lanes if head == 0 else ~low_lanes
+        my_q, my_k, my_do = (jnp.where(here, t, zero) for t in (q, k, do))
+        delta = jnp.sum(jnp.where(here, product, 0.0), axis=1, keepdims=True)
+        p = p_ref[head]
+        dp = dot(my_do, v, NT)
+        ds = (p.astype(F32) * (dp - delta)).astype(BF16)
+        dq = dq + dot(ds, my_k)
+        dk = dk + dot(ds, my_q, (((0,), (0,)), ((), ())))
+        dv = dv + dot(p, my_do, (((0,), (0,)), ((), ())))
+    return (dq * scale).astype(BF16), dk.astype(BF16), dv.astype(BF16)
+
+
+def attend_back_body(scale, q_ref, k_ref, v_ref, p_ref, att_ref, do_ref, out_ref):
+    parts = attend_back_one(
+        scale, q_ref[0], k_ref[0], v_ref[0], p_ref, att_ref[...], do_ref[...]
+    )
+    for i in range(3):
+        out_ref[i] = parts[i]
+
+
+def attend_back_shared_body(
+    scale, mine_ref, mate_ref, p_ref, att_keep, att_send, do_keep, do_mate, keep_ref, send_ref
+):
+    q, k, v = (jnp.concatenate([mine_ref[i], mate_ref[i]]) for i in range(3))
+    att = jnp.concatenate([att_keep[...], att_send[...]])
+    do = jnp.concatenate([do_keep[...], do_mate[...]])
+    parts = attend_back_one(scale, q, k, v, p_ref, att, do)
+    count = keep_ref.shape[1]
+    for i in range(3):
+        keep_ref[i] = parts[i][:count]
+        send_ref[i] = parts[i][count:]
+
+
+def out_body(
+    place, own_ref, keep_ref, mate_ref, x_ref, r0, r1, r2, r3, a_ref, b_ref, bias_ref, gain,
+    lbias, aup_ref, sel_ref, hid_ref, z_ref, u_ref, uup_ref, w_ref,
+):
+    width = x_ref.shape[1]
+    half = width // 2
+
+    @pl.when(pl.program_id(0) == 0)
+    def _():
+        settle_out(place, (r0, r1, r2, r3), w_ref)
+
+    keep, mate = keep_ref[...], mate_ref[...]
+    shared = jnp.concatenate(
+        [chosen(place[2], keep, mate), chosen(place[2], mate, keep)], axis=1
+    )
+    att = jnp.where(pl.program_id(0) < 2, own_ref[...], shared)
+    sel = sel_ref[...]
+    low = dot(att[:, :half], a_ref[0], NT) + dot(att[:, half:], a_ref[1], NT)
+    kept = (low * sel).astype(BF16)
+    u_ref[...] = kept
+    acc = dot(att, w_ref[...].reshape(width, width), NT) + dot(kept, b_ref[...])
+    hidden = x_ref[...].astype(F32) + acc + bias_ref[...]
+    hid_ref[...] = hidden
+    normal, _ = norm_of(hidden)
+    z = (normal * gain[...] + lbias[...]).astype(BF16)
+    z_ref[...] = z
+    uup_ref[...] = (dot(z, aup_ref[...]) * sel).astype(BF16)
+
+
+def mlp_body(
+    rows, place, z_ref, gown_ref, gnear_ref, gfar_ref, uup_ref, sel_ref, hid_ref, wup_ref,
+    wdn_ref, bup_own, bup_near, bup_far, adn_own, adn_near, adn_far, upb_ref, bdn_ref, aup_ref,
+    dnb_ref, gain,
+    own_ref, near_ref, far_ref, gh_ref, ghb_ref, ekeep_ref, esend_ref,
+    down_acc, dz_acc, udn_acc, eup_acc, edn_ref, uup_t, edn_t, act_ref, dup_ref, gy_ref,
+):
+    total, width = z_ref.shape
+    step = pl.program_id(0)
+    blocks = [slice(i, i + rows) for i in range(0, total, rows)]
+
+    @pl.when(step == 0)
+    def _():
+        for b in blocks:
+            left, right = both_halves(place, gown_ref[b, :], gnear_ref[b, :], gfar_ref[b, :])
+            gy = jnp.concatenate([left, right], axis=1)
+            gy_ref[b, :] = gy
+            edn_ref[b, :] = (dot(gy, bdn_ref[...], NT) * sel_ref[b, :]).astype(BF16)
+        edn_t[...] = edn_ref[...].T
+        uup_t[...] = uup_ref[...].T
+        down_acc[...] = jnp.zeros_like(down_acc)
+        dz_acc[...] = jnp.zeros_like(dz_acc)
+        udn_acc[...] = jnp.zeros_like(udn_acc)
+        eup_acc[...] = jnp.zeros_like(eup_acc)
+
+    chunk = upb_ref.shape[1]
+    wup = wup_ref[...].reshape(width, chunk)
+    wdn = wdn_ref[...].reshape(width, chunk)
+    parts = pl.num_programs(0) // 2
+    y = step // parts
+
+    def adapter(own_ref, near_ref, far_ref):
+        near, far = near_ref[...], far_ref[...]
+        other = jnp.concatenate([chosen(place[2], near, far), chosen(place[2], far, near)])
+        return jnp.where(place[3] == y, own_ref[...], other)
+
+    bup = adapter(bup_own, bup_near, bup_far)
+    adn = adapter(adn_own, adn_near, adn_far)
+    for b in blocks:
+        pre = dot(z_ref[b, :], wup) + dot(uup_ref[b, :], bup) + upb_ref[...]
+        q = 1.0 / (1.0 + jnp.exp(-GELU_SCALE * pre))
+        act = (pre * q).astype(BF16)
+        d_act = dot(gy_ref[b, :], wdn) + dot(edn_ref[b, :], adn)
+        d_up = (d_act * (q + GELU_SCALE * pre * q * (1.0 - q))).astype(BF16)
+        act_ref[b, :] = act
+        dup_ref[b, :] = d_up
+        down_acc[b, :] += dot(act, wdn, NT)
+        dz_acc[b, :] += dot(d_up, wup, NT)
+        udn_acc[b, :] += dot(act, adn, NT)
+        eup_acc[b, :] += dot(d_up, bup, NT)
+    hidden_half = parts * chunk
+    for i, (low, high) in enumerate(((uup_t, dup_ref), (edn_t, act_ref))):
+        rows = split_rows(place, dot(low[...], high[...]).astype(BF16))
+        lanes = pl.ds(pl.multiple_of(i * hidden_half + step % parts * chunk, chunk), chunk)
+        ekeep_ref[y, :, lanes], esend_ref[y, :, lanes] = rows
+
+    @pl.when(step == pl.num_programs(0) - 1)
+    def _():
+        gbdn = gaup = 0.0
+        for b in blocks:
+            sel = sel_ref[b, :]
+            e_up = (eup_acc[b, :] * sel).astype(BF16)
+            u_dn = (udn_acc[b, :] * sel).astype(BF16)
+            hidden = hid_ref[b, :]
+            y = hidden + down_acc[b, :] + dot(u_dn, bdn_ref[...]) + dnb_ref[...]
+            halves_out(place, y.astype(BF16), b, own_ref, near_ref, far_ref)
+            dz = dz_acc[b, :] + dot(e_up, aup_ref[...], NT)
+            normal, inverse = norm_of(hidden)
+            grad = gy_ref[b, :].astype(F32) + norm_pull(dz, normal, inverse, gain[...])
+            gh_ref[b, :] = grad
+            ghb_ref[b, :] = grad.astype(BF16)
+            gbdn = gbdn + dot_rows(u_dn, gy_ref[b, :])
+            gaup = gaup + dot_rows(e_up, z_ref[b, :])
+        half = width // 2
+        for i, grad in enumerate((gaup, gbdn)):
+            start = 2 * hidden_half + i * half
+            for column in range(2):
+                rows = split_rows(place, grad[:, column * half : (column + 1) * half].astype(BF16))
+                lanes = slice(start, start + half)
+                ekeep_ref[column, :, lanes], esend_ref[column, :, lanes] = rows
+
+
+def split_rows(place, grad):
+    part = grad.shape[0] // 2
+    low, high = grad[:part], grad[part:]
+    return chosen(place[2], low, high), chosen(place[2], high, low)
+
+
+def out_back_body(
+    place, g_ref, own_ref, keep_ref, mate_ref, r0, r1, r2, r3, a_ref, b_ref, sel_ref, u_ref,
+    d_own, d_keep, d_send, g_keep, g_send, w_ref, e_ref, e_t,
+):
+    width = g_ref.shape[1]
+    half = width // 2
+    count = keep_ref.shape[0]
+    y = pl.program_id(0)
+
+    @pl.when(y == 0)
+    def _():
+        def store(row, column, block):
+            w_ref[column, row] = block
+
+        settle(place, (r0, r1, r2, r3), True, store)
+        e = (dot(g_ref[...], b_ref[...], NT) * sel_ref[...]).astype(BF16)
+        e_ref[...] = e
+        e_t[...] = e.T
+        gb = dot(u_ref[...].T, g_ref[...]).astype(BF16)
+        for column in range(2):
+            rows = split_rows(place, gb[:, column * half : (column + 1) * half])
+            g_keep[column, :, half:], g_send[column, :, half:] = rows
+
+    w = w_ref[y].reshape(width, half)
+    d = (dot(g_ref[...], w) + dot(e_ref[...], a_ref[0])).astype(BF16)
+    d_own[...] = d[: 2 * count]
+
+    shared = jnp.where(place[2] == y, keep_ref[...], mate_ref[...])
+    ga = dot(e_t[...], jnp.concatenate([own_ref[...], shared])).astype(BF16)
+    g_keep[y, :, :half], g_send[y, :, :half] = split_rows(place, ga)
+
+    @pl.when(place[2] == y)
+    def _():
+        d_keep[...] = d[2 * count :]
+
+    @pl.when(place[2] != y)
+    def _():
+        d_send[...] = d[2 * count :]
+
+
+def whole_rows(place, own, keep, mate):
+    shared = jnp.concatenate(
+        [chosen(place[2], keep, mate), chosen(place[2], mate, keep)], axis=1
+    )
+    return jnp.concatenate([own, shared])
+
+
+def qkv_grads_body(
+    place, own_ref, keep_ref, mate_ref, b_ref, sel_ref, u_ref, z_ref, e_ref, keep_out, send_out
+):
+    width = z_ref.shape[1]
+    half = width // 2
+    stack = sel_ref.shape[1]
+    part = stack // 2
+    d = whole_rows(place, own_ref[0], keep_ref[0], mate_ref[0])
+    u_t = u_ref[...].T
+    low = dot(d[:, :half], b_ref[0], NT) + dot(d[:, half:], b_ref[1], NT)
+    e = (low * sel_ref[...]).astype(BF16)
+    e_ref[...] = e
+    gb = dot(u_t, d).astype(BF16)
+    ga = dot(e.T, z_ref[...]).astype(BF16)
+    for y in range(2):
+        for i, grad in enumerate((gb, ga)):
+            low_rows, high_rows = (
+                grad[r * part : (r + 1) * part, y * half : (y + 1) * half] for r in range(2)
+            )
+            keep_out[y, i, 0] = chosen(place[2], low_rows, high_rows)
+            send_out[y, i, 0] = chosen(place[2], high_rows, low_rows)
+
+
+def qkv_back_body(
+    place, own_ref, keep_ref, mate_ref, p0, p1, p2, p3, r0, r1, r2, r3, a_ref, e_ref, x_ref,
+    gh_ref, gain, own_out, near_out, far_out, w_ref,
+):
+    width = x_ref.shape[1]
+    step = pl.program_id(0)
+
+    @pl.when(step == 0)
+    def _():
+        settle_qkv(place, (p0, p1, p2, p3), (r0, r1, r2, r3), w_ref)
+
+    dz = dot(e_ref[...], a_ref[...], NT)
+    for k in range(3):
+        keep, mate = keep_ref[k], mate_ref[k]
+        shared = jnp.concatenate(
+            [chosen(place[2], keep, mate), chosen(place[2], mate, keep)], axis=1
+        )
+        d = jnp.where(step < 2, own_ref[k], shared)
+        dz = dz + dot(d, w_ref[k].reshape(width, width), NT)
+    normal, inverse = norm_of(x_ref[...].astype(F32))
+    grad = gh_ref[...] + norm_pull(dz, normal, inverse, gain[...])
+    halves_out(place, grad.astype(BF16), slice(None), own_out, near_out, far_out)
+
+
+def on_chip_pair(
+    mesh_shape, tokens, cotangent, ln1_gain, ln1_bias, ln2_gain, ln2_bias, w_qkv, qv_bias, w_out,
+    out_bias, w_up, up_bias, w_down, down_bias, adapter_ids, a_qkv, b_qkv, a_out, b_out, a_up,
+    b_up, a_down, b_down,
+):
+    n_row, n_col = mesh_shape
+    count, half = tokens.shape
+    width = half * 2
+    stack = b_out.shape[0]
+    part = stack // 2
+    hidden_half = w_up.shape[1]
+    hidden = hidden_half * 2
+    length = count // adapter_ids.shape[0]
+    cut = length // 2
+    heads = width // HD
+    tb = -(-(length + 1) // 32) * 16
+    own_rows, total = 2 * tb, 3 * tb
+    scale = HD ** (-0.5)
+    both = ("row", "col")
+    row, col = lax.axis_index("row"), lax.axis_index("col")
+    core, side, n_far = row % 2, row // 2 % 2, n_row // 4
+    place = jnp.stack([row // 4, side, core, col]).astype(jnp.int32)
+
+    def device(r, c):
+        return r * n_col + c
+
+    far_swaps = [[] for _ in range(n_far.bit_length() - 1)]
+    far_turns = [[] for _ in range(n_far - 1)]
+    ring_in, ring_back, cross, cores, cols_swap, sides_swap = [], [], [], [], [], []
+    for r in range(n_row):
+        for c in range(n_col):
+            k, mate = r % 2, r + 1 - 2 * (r % 2)
+            cores.append((device(r, c), device(mate, c)))
+            cols_swap.append((device(r, c), device(r, 1 - c)))
+            sides_swap.append((device(r, c), device(r ^ 2, c)))
+            for turn, pairs in enumerate(far_turns):
+                pairs.append((device(r, c), device((r + 4 * (turn + 1)) % n_row, c)))
+            for bit, pairs in enumerate(far_swaps):
+                pairs.append((device(r, c), device(r ^ (4 << bit), c)))
+            if k != c:
+                ring_in.append((device(r, c), device(r, 1 - c)))
+                ring_back.append((device(r, c), device(mate, c)))
+                cross.append((device(r, c), device(mate, 1 - c)))
+            else:
+                ring_in.append((device(r, c), device(mate, c)))
+                ring_back.append((device(r, c), device(r, 1 - c)))
+
+    def move(values, pairs):
+        return lax.ppermute(values, both, pairs)
+
+    def pick(pair, index):
+        return jnp.where(index == 0, pair[0], pair[1])
+
+    def ordered(mine, other, index, axis):
+        return jnp.where(
+            index == 0,
+            jnp.concatenate([mine, other], axis),
+            jnp.concatenate([other, mine], axis),
+        )
+
+    def tie(*values):
+        return lax.optimization_barrier(values)
+
+    thirds = [struct((total, half), BF16)] * 3
+    third_specs = [fixed((total, half))] * 3
+
+    def spread(values):
+        return call(
+            functools.partial(spread_body, length, cut, own_rows, tb),
+            (1,),
+            [SPOT, fixed((count, half))],
+            third_specs,
+            thirds,
+            scratch=[pltpu.VMEM((count, half), F32)],
+        )(place, values)
+
+    def join(own, near, far, kind):
+        return call(
+            functools.partial(join_body, length, cut, own_rows),
+            (1,),
+            [SPOT] + third_specs,
+            fixed((count, half)),
+            struct((count, half), kind),
+            scratch=[pltpu.VMEM((count, half), F32)],
+        )(place, own, near, far)
+
+    x_own, x_near, x_far = spread(tokens)
+    x_near, x_far, w_qkv, w_out = tie(x_near, x_far, w_qkv, w_out)
+    mine_first = jnp.concatenate(
+        [jnp.swapaxes(w_qkv, 0, 1).reshape(-1, 3 * half), w_out.T], axis=1
+    )
+    mine_second = jnp.concatenate([w_up, w_down.T], axis=1)
+    adapt_first = jnp.concatenate(
+        [jnp.swapaxes(b_qkv, 0, 1).reshape(stack, 3 * half), a_out.T], axis=1
+    )
+    adapt_second = jnp.concatenate([b_up, a_down.T], axis=1)
+    deep = width // n_row
+
+    def turned(block):
+        return jnp.stack([block] + [move(block, pairs) for pairs in far_turns])
+
+    def doubled(found, pairs):
+        return jnp.concatenate([found, move(found, pairs)])
+
+    def part_of(values):
+        return lax.dynamic_slice_in_dim(values, core * part, part, 0)
+
+    def widened(values, near, far):
+        return ordered(values[None], ordered(near, far, core, 0)[None], col, 0)
+
+    x_near, x_far = move(x_near, ring_in), move(x_far, cross)
+    near0, near1 = turned(mine_first[:, :width]), turned(mine_first[:, width:])
+    near0, near1, x_near, x_far, mine_second = tie(near0, near1, x_near, x_far, mine_second)
+    x_parts = (x_own, x_near, x_far)
+    big_second = lax.all_gather(mine_second, both, axis=0, tiled=False)
+    big_second = big_second.reshape(n_row, n_col, deep, 2 * hidden_half)
+    near0, near1 = doubled(near0, sides_swap), doubled(near1, cols_swap)
+    ad_near = move(part_of(adapt_first), cols_swap)
+    biases = jnp.concatenate([qv_bias[0], qv_bias[1], up_bias])[None]
+    bias_pair = ordered(biases, move(biases, cols_swap), col, 0)
+    ids = jnp.where(core == col, adapter_ids, move(adapter_ids, cores))
+    g_own, g_near, g_far = spread(cotangent)
+    near0, near1, bias_pair, ids, ad_near = tie(near0, near1, bias_pair, ids, ad_near)
+    ad_first = widened(adapt_first, ad_near, move(ad_near, cores))
+    last0, last1 = move(near0, cols_swap), move(near1, sides_swap)
+    far0, far1 = move(near0, cores), move(near1, cores)
+    last0, last1, far0, far1, ad_first, g_near, g_far = tie(
+        last0, last1, far0, far1, ad_first, g_near, g_far
+    )
+    blocks0 = (near0, last0, far0, move(last0, cores))
+    blocks1 = (near1, last1, far1, move(last1, cores))
+    qv_rows = jnp.stack(
+        [
+            bias_pair[:, :half].reshape(1, width),
+            jnp.zeros((1, width), F32),
+            bias_pair[:, half:width].reshape(1, width),
+        ]
+    )
+    up_row = bias_pair[:, width:].reshape(1, hidden)
+
+    owners = lax.iota(jnp.int32, stack) // RANK
+    own_id = jnp.where(core == 0, ids[0], ids[2])
+    places = lax.iota(jnp.int32, total)[:, None]
+    sel = (jnp.where(places < own_rows, own_id, ids[1]) == owners[None]).astype(F32)
+
+    valid = jnp.arange(own_rows)[:, None]
+    here, there = jnp.where(core == 0, cut, length - cut), jnp.where(core == 0, length - cut, cut)
+
+    def mask_of(good):
+        return jnp.broadcast_to(jnp.where(good, 0.0, -1e30), (own_rows, 2 * HD)).astype(BF16)
+
+    mask_own = mask_of(valid < length)
+    mask_shared = mask_of((valid < here) | ((valid >= tb) & (valid < tb + there)))
+
+    gain1, bias1, gain2, bias2 = (t[None] for t in (ln1_gain, ln1_bias, ln2_gain, ln2_bias))
+
+    rows_block = pl.BlockSpec((tb, width), lambda i: (i, 0))
+    sel_block = pl.BlockSpec((tb, stack), lambda i: (i, 0))
+    every = fixed((total, width))
+    thin = fixed((total, stack))
+    vec = fixed((1, width))
+    pieces0 = [fixed((n_row // 2, deep, width))] * 4
+    pieces1 = [fixed((n_row // 2, deep, half))] * 4
+    pieces_out = [
+        pl.BlockSpec(
+            (n_row // 2, deep, half), lambda *_: (0, 0, 1), pipeline_mode=pl.Buffered(1)
+        )
+    ] * 4
+    w_qkv_room = [pltpu.VMEM((3, n_row, deep, width), BF16)]
+    w_out_room = [pltpu.VMEM((n_row, deep, width), BF16)]
+    ad_out_spec = pl.BlockSpec(
+        (n_col, stack, half), lambda *_: (0, 0, 3), pipeline_mode=pl.Buffered(1)
+    )
+    low_k = pl.BlockSpec((total, stack), lambda k: (0, k))
+    own_k = pl.BlockSpec((1, own_rows, width), lambda k: (k, 0, 0))
+    shared_k = pl.BlockSpec((1, tb, half), lambda k: (k, 0, 0))
+    ad_k = pl.BlockSpec((n_col, stack, half), lambda k: (0, 0, k))
+    shared_struct = struct((3, tb, half), BF16)
+    half_rows = struct((tb, half), BF16)
+
+    third_rows = pl.BlockSpec((tb, half), lambda i: (i, 0))
+    low_block = pl.BlockSpec((tb, 3 * stack), lambda i: (i, 0))
+    own_three = pl.BlockSpec((3, tb, width), lambda i: (0, jnp.minimum(i, 1), 0))
+    all_three = pl.BlockSpec((3, tb, width), lambda i: (0, i, 0))
+    shared_three = fixed((3, tb, half))
+    x, z1, u_qkv, qkv, qkv_keep, qkv_send = call(
+        functools.partial(qkv_body, scale),
+        (3,),
+        [
+            SPOT, third_rows, third_rows, third_rows, vec, vec, *pieces0, *pieces1,
+            fixed((width, 3 * stack)),
+            pl.BlockSpec(
+                (n_col, stack, 3 * half), lambda i: (0, 0, 0), pipeline_mode=pl.Buffered(1)
+            ),
+            fixed((3, 1, width)), sel_block,
+        ],
+        [rows_block, rows_block, low_block, all_three, shared_three, shared_three],
+        [
+            struct((total, width), BF16),
+            struct((total, width), BF16),
+            struct((total, 3 * stack), BF16),
+            struct((3, total, width), BF16),
+            shared_struct,
+            shared_struct,
+        ],
+        scratch=w_qkv_room,
+    )(place, *x_parts, gain1, bias1, *blocks0, *blocks1, a_qkv, ad_first, qv_rows, sel)
+
+    qkv_mate = move(qkv_send, cores)
+    adapt_part = part_of(adapt_second)
+    qkv, g_near, g_far, adapt_part = tie(qkv, g_near, g_far, adapt_part)
+    g_near, g_far = move(g_near, ring_in), move(g_far, cross)
+    ad_near = move(adapt_part, cols_swap)
+
+    head_specs = [pl.BlockSpec((1, own_rows, 2 * HD), lambda h, k=k: (k, 0, h)) for k in range(3)]
+    head_rows = pl.BlockSpec((own_rows, 2 * HD), lambda h: (0, h))
+    head_p = pl.BlockSpec((2, own_rows, own_rows), lambda h: (h, 0, 0))
+    pair_k = pl.BlockSpec((3, tb, 2 * HD), lambda h: (0, 0, h))
+    pair_rows = pl.BlockSpec((tb, 2 * HD), lambda h: (0, h))
+    att_own, p_own = call(
+        attend_body,
+        (heads // 2,),
+        head_specs + [fixed((own_rows, 2 * HD))],
+        [head_rows, head_p],
+        [struct((own_rows, width), BF16), struct((heads, own_rows, own_rows), BF16)],
+    )(qkv, qkv, qkv, mask_own)
+    qkv_mate, att_own = tie(qkv_mate, att_own)
+    att_keep, att_send, p_sh = call(
+        attend_shared_body,
+        (heads // 4,),
+        [pair_k, pair_k, fixed((own_rows, 2 * HD))],
+        [pair_rows, pair_rows, head_p],
+        [half_rows, half_rows, struct((heads // 2, own_rows, own_rows), BF16)],
+    )(qkv_keep, qkv_mate, mask_shared)
+    att_mate = move(att_send, cores)
+    att_mate, ad_near, g_near, g_far = tie(att_mate, ad_near, g_near, g_far)
+    g_parts = (g_own, g_near, g_far)
+    ad_second = (adapt_second, ad_near, move(ad_near, cores))
+
+    own_block = pl.BlockSpec((tb, width), lambda i: (jnp.minimum(i, 1), 0))
+    shared_rows = fixed((tb, half))
+    hid, z2, u_out, u_up = call(
+        out_body,
+        (3,),
+        [
+            SPOT, own_block, shared_rows, shared_rows, rows_block, *pieces_out,
+            ad_out_spec, fixed((stack, width)), vec, vec, vec, fixed((width, stack)), sel_block,
+        ],
+        [rows_block, rows_block, sel_block, sel_block],
+        [
+            struct((total, width), F32),
+            struct((total, width), BF16),
+            struct((total, stack), BF16),
+            struct((total, stack), BF16),
+        ],
+        scratch=w_out_room,
+    )(
+        place, att_own, att_keep, att_mate, x, *blocks1, ad_first, b_out, out_bias[None],
+        gain2, bias2, a_up, sel,
+    )
+
+    chunk = half
+    parts = hidden_half // chunk
+
+    def w_spec(shift):
+        return pl.BlockSpec(
+            (n_row, 1, deep, chunk), lambda j: (0, j // parts, 0, j % parts + shift)
+        )
+
+    def ad_specs(shift):
+        return [
+            pl.BlockSpec((rows, chunk), lambda j: (0, j % parts + shift))
+            for rows in (stack, part, part)
+        ]
+
+    early_half = fixed((2, part, 2 * hidden_half + 2 * half))
+    early_struct = struct((2, part, 2 * hidden_half + 2 * half), BF16)
+    y_own, y_near, y_far, g_h, ghb, early_keep, early_send = call(
+        functools.partial(mlp_body, tb),
+        (2 * parts,),
+        [SPOT, every]
+        + third_specs
+        + [
+            thin, thin, every, w_spec(0), w_spec(parts), *ad_specs(0), *ad_specs(parts),
+            pl.BlockSpec((1, chunk), lambda j: (0, j)), fixed((stack, width)),
+            fixed((width, stack)), vec, vec,
+        ],
+        third_specs + [every, every, early_half, early_half],
+        thirds
+        + [struct((total, width), F32), struct((total, width), BF16), early_struct, early_struct],
+        scratch=[
+            pltpu.VMEM((total, width), F32),
+            pltpu.VMEM((total, width), F32),
+            pltpu.VMEM((total, stack), F32),
+            pltpu.VMEM((total, stack), F32),
+            pltpu.VMEM((total, stack), BF16),
+            pltpu.VMEM((stack, total), BF16),
+            pltpu.VMEM((stack, total), BF16),
+            pltpu.VMEM((total, chunk), BF16),
+            pltpu.VMEM((total, chunk), BF16),
+            pltpu.VMEM((total, width), BF16),
+        ],
+    )(
+        place, z2, *g_parts, u_up, sel, hid, big_second, big_second, *ad_second, *ad_second, up_row,
+        b_down, a_up, down_bias[None], gain2,
+    )
+
+    def added(kept, sent):
+        return (kept.astype(F32) + sent.astype(F32)).astype(BF16)
+
+    quarter = part // 2
+
+    def quarter_of(values, index):
+        return lax.dynamic_slice_in_dim(values, index * quarter, quarter, 1)
+
+    def side_sent(values):
+        return move(quarter_of(values, 1 - side), sides_swap)
+
+    early_sum = added(early_keep, move(early_send, cores))
+    early_sum, ghb = tie(early_sum, ghb)
+    early_sent = side_sent(early_sum)
+    out_half = fixed((2, part, width))
+    d_att, d_keep, d_send, out_keep, out_send = call(
+        out_back_body,
+        (2,),
+        [
+            SPOT, every, pl.BlockSpec((own_rows, half), lambda i: (0, i)), shared_rows,
+            shared_rows, *pieces_out,
+            pl.BlockSpec((1, stack, half), lambda i: (i, 0, 3)), fixed((stack, width)), thin, thin,
+        ],
+        [
+            pl.BlockSpec((own_rows, half), lambda i: (0, i)), shared_rows, shared_rows, out_half,
+            out_half,
+        ],
+        [
+            struct((own_rows, width), BF16),
+            half_rows,
+            half_rows,
+            struct((2, part, width), BF16),
+            struct((2, part, width), BF16),
+        ],
+        scratch=[
+            pltpu.VMEM((2, n_row, deep, half), BF16),
+            pltpu.VMEM((total, stack), BF16),
+            pltpu.VMEM((stack, total), BF16),
+        ],
+    )(place, ghb, att_own, att_keep, att_mate, *blocks1, ad_first, b_out, sel, u_out)
+
+    d_mate = move(d_send, cores)
+    out_sum = added(out_keep, move(out_send, cores))
+    d_mate, out_sum = tie(d_mate, out_sum)
+    out_sent = side_sent(out_sum)
+
+    g_keep, g_send = call(
+        functools.partial(attend_back_shared_body, scale),
+        (heads // 4,),
+        [pair_k, pair_k, head_p, pair_rows, pair_rows, pair_rows, pair_rows],
+        [pair_k, pair_k],
+        [shared_struct, shared_struct],
+    )(qkv_keep, qkv_mate, p_sh, att_keep, att_send, d_keep, d_mate)
+    early_sum = jnp.concatenate(
+        [
+            added(quarter_of(early_sum, side), early_sent),
+            added(quarter_of(out_sum, side), out_sent),
+        ],
+        axis=2,
+    )
+    d_att, g_send, y_near, y_far, early_sum = tie(d_att, g_send, y_near, y_far, early_sum)
+    early_sent = move(pick(early_sum, 1 - col), cols_swap)
+    g_mate = move(g_send, cores)
+    y_near, y_far = move(y_near, ring_back), move(y_far, cross)
+    d_own = call(
+        functools.partial(attend_back_body, scale),
+        (heads // 2,),
+        head_specs + [head_p, head_rows, head_rows],
+        pl.BlockSpec((3, own_rows, 2 * HD), lambda h: (0, 0, h)),
+        struct((3, own_rows, width), BF16),
+    )(qkv, qkv, qkv, p_own, att_own, d_att)
+
+    grad_spec = pl.BlockSpec((2, 2, 1, part, half), lambda k: (0, 0, k, 0, 0))
+    grad_struct = struct((2, 2, 3, part, half), BF16)
+    early_sum = added(pick(early_sum, col), early_sent)
+    d_own, early_sum = tie(d_own, early_sum)
+    early_sent = move(early_sum, far_swaps[0])
+    e_qkv, q_kept, q_sent = call(
+        qkv_grads_body,
+        (3,),
+        [SPOT, own_k, shared_k, shared_k, ad_k, thin, low_k, every],
+        [low_k, grad_spec, grad_spec],
+        [struct((total, 3 * stack), BF16), grad_struct, grad_struct],
+    )(place, d_own, g_keep, g_mate, ad_first, sel, u_qkv, z1)
+
+    def side_of(values, index):
+        return jnp.where(index == 0, values[:, 0], values[:, 1])
+
+    sums = added(q_kept, move(q_sent, cores)).reshape(2, 2, 3 * part, half)
+    early_sum = added(early_sum, early_sent)
+    sums, d_own, e_qkv, early_sum = tie(sums, d_own, e_qkv, early_sum)
+    early_sent = move(early_sum, far_swaps[-1])
+    q_sent = move(side_of(sums, 1 - side), sides_swap)
+    t_own, t_near, t_far = call(
+        qkv_back_body,
+        (3,),
+        [
+            SPOT, own_three, shared_three, shared_three, *pieces0, *pieces1,
+            fixed((width, 3 * stack)), low_block, rows_block, rows_block, vec,
+        ],
+        [third_rows, third_rows, third_rows],
+        thirds,
+        scratch=w_qkv_room,
+    )(place, d_own, g_keep, g_mate, *blocks0, *blocks1, a_qkv, e_qkv, x, g_h, gain1)
+    sums = added(side_of(sums, side), q_sent)
+    early_sum = added(early_sum, early_sent)
+    sums, t_near, t_far, y_near, y_far, early_sum = tie(
+        sums, t_near, t_far, y_near, y_far, early_sum
+    )
+    q_sent = move(pick(sums, 1 - col), cols_swap)
+    t_near, t_far = move(t_near, ring_back), move(t_far, cross)
+    layer_out = join(y_own, y_near, y_far, BF16)
+    edge = 2 * hidden_half
+    whole = edge + 4 * half
+    split_lanes = [slice(edge, edge + 2 * half), slice(edge + 3 * half, whole)]
+    rest = jnp.concatenate([early_sum[:, lanes] for lanes in split_lanes], axis=1)
+    early_sum = jnp.concatenate([early_sum, move(rest, cols_swap)], axis=1)
+    q_sent, layer_out, early_sum = tie(q_sent, layer_out, early_sum)
+    early_sent = move(early_sum, sides_swap)
+    sums = added(pick(sums, col), q_sent)
+    for pairs in far_swaps[:-1]:
+        sums = added(sums, move(sums, pairs))
+    q_sent = move(sums, far_swaps[-1])
+    early_sum = ordered(early_sum, early_sent, side, 0)
+    q_sent, t_near, t_far, early_sum = tie(q_sent, t_near, t_far, early_sum)
+    early_sent = move(early_sum, cores)
+    sums = added(sums, q_sent)
+    sums = ordered(sums[None], move(sums, sides_swap)[None], side, 0)
+    a_sent = move(sums[1:], cols_swap)
+    tokens_grad = join(t_own, t_near, t_far, F32)
+    mine = ordered(early_sum, early_sent, core, 0).astype(F32)
+    a_sent, tokens_grad, mine = tie(a_sent, tokens_grad, mine)
+    every_sum = jnp.concatenate([sums[:1], ordered(sums[1:], a_sent, col, 0)])
+    every_sum = every_sum.reshape(3, 3, part, half)
+    every_sum = ordered(every_sum, move(every_sum, cores), core, 2).reshape(3, 3 * stack, half)
+    b_sum = every_sum[0].reshape(3, stack, half).astype(F32)
+    a_sum = jnp.concatenate([every_sum[1].T, every_sum[2].T]).astype(F32)
+
+    own_starts = (edge, edge + half, edge + 3 * half)
+    a_up_sum, b_down_sum, b_out_sum = (
+        ordered(
+            mine[:, start : start + half],
+            mine[:, whole + i * half : whole + (i + 1) * half],
+            col,
+            1,
+        )
+        for i, start in enumerate(own_starts)
+    )
+    return (
+        layer_out,
+        tokens_grad,
+        a_sum,
+        b_sum,
+        mine[:, edge + 2 * half : edge + 3 * half].T,
+        b_out_sum,
+        a_up_sum.T,
+        mine[:, :hidden_half],
+        mine[:, hidden_half:edge].T,
+        b_down_sum,
+    )
+
+
 def solution(mesh):
     placed = (
         P("row", "col"),
@@ -230,8 +1166,10 @@
         P("col", None),
         P(),
     )
+    shape = (mesh.shape["row"], mesh.shape["col"])
+    paired = shape[1] == 2 and shape[0] >= 16 and shape[0] & (shape[0] - 1) == 0
     return jax.shard_map(
-        on_device,
+        functools.partial(on_chip_pair, shape) if paired else on_device,
         mesh=mesh,
         in_specs=placed,
         out_specs=(

time: 1180 us -> 431 us (0.37)
  waiting for transfers between devices: 649 us -> 117 us
  matrix products: 270 us -> 0 us
  Pallas kernels: 0 us -> 194 us
  local copies, waits for them, and re-layouts: 122 us -> 17.7 us
  other arithmetic: 82.1 us -> 27.5 us
  starting transfers between devices: 1.14 us -> 50.4 us
  blocking collectives: 30.3 us -> 0 us
    all_gather x8 -> x1, waiting for transfers between devices: 292 us -> 0.02 us  [on_chip_pair(): big_second = lax.all_gather(mine_second, both, axis=0, tiled=False)]
    dot_general x38 -> x0, matrix products: 270 us -> none  [mult(): return jnp.einsum(form, first, second, preferred_element_type=jnp.float32)]
    psum x2 -> x0, waiting for transfers between devices: 201 us -> none  [the longest x1 131 us: on_device(): lax.psum((grad_a_qkv, grad_b_out, grad_a_up, grad_b_down), ('row', 'col'))]
    pallas_call x0 -> x14, Pallas kernels: none -> 194 us  [the longest x1 61.2 us: on_chip_pair(): call(functools.partial(mlp_body, tb), (2 * parts,), [SPOT, every] + third...]
    reduce_scatter x4 -> x0, waiting for transfers between devices: 153 us -> none  [sum_partials(): lax.psum_scatter(terms.astype(jnp.bfloat16), 'col', scatter_dimension=1,...]
    ppermute x0 -> x50, waiting for transfers between devices: none -> 117 us  [move(): return lax.ppermute(values, both, pairs)]
    ppermute x0 -> x50, starting transfers between devices: none -> 50.3 us  [move(): return lax.ppermute(values, both, pairs)]
    convert_element_type x10 -> x18, other arithmetic: 51.1 us -> 9.54 us  [the longest x12 5.84 us: added(): return (kept.astype(F32) + sent.astype(F32)).astype(BF16)]
  transfers between devices with their start and end apart: 14 -> 51, of which waited for: 13 -> 21; matrix products, arithmetic and copies ran while one was open for 19% -> 7% of each run, Pallas kernels for 0% -> 28%
where the time goes in v1:
time: 431 us; the launch traced here: 422 us
  Pallas kernels  194 us (45%)
  waiting for transfers between devices  117 us (27%)
  starting transfers between devices  50.4 us (12%)
  other arithmetic  27.5 us (6%)
  local copies, waits for them, and re-layouts  17.7 us (4%)
  between operations  16.4 us (4%)
    ppermute x50, waiting for transfers between devices, move(): return lax.ppermute(values, both, pairs)  117 us
    pallas_call x1, Pallas kernels, on_chip_pair(): call(functools.partial(mlp_body, tb), (2 * parts,), [SPOT, every] + third...  61.2 us
    ppermute x50, starting transfers between devices, move(): return lax.ppermute(values, both, pairs)  50.3 us
    pallas_call x1, Pallas kernels, on_chip_pair(): call(attend_body, (heads // 2,), head_specs + [fixed((own_rows, 2 * HD))]...  18.1 us
    pallas_call x1, Pallas kernels, on_chip_pair(): call(functools.partial(attend_back_body, scale), (heads // 2,), head_spec...  17.9 us
    pallas_call x1, Pallas kernels, on_chip_pair(): call(functools.partial(qkv_body, scale), (3,), [SPOT, third_rows, third_r...  16.9 us
    pallas_call x1, Pallas kernels, on_chip_pair(): call(qkv_back_body, (3,), [SPOT, own_three, shared_three, shared_three, *...  15.4 us
    unnamed x80, local copies, waits for them, and re-layouts  11.1 us
  transfers between devices with their start and end apart: 51, of which 21 were waited for; matrix products, arithmetic and copies ran while one was open for 7% of the time, Pallas kernels for 28%

profile of v1, /device:TPU:0, one launch (start us, length us, event | category | flops | bytes accessed | tf_op | source)
XLA Modules:
  0.0 422.3 jit_solution(15180686813535989464)
XLA Ops:
  8.0 4.0 shard_map.294
  13.2 2.6 collective-permute-start.3
  15.8 2.6 collective-permute-start.4
  18.4 1.3 collective-permute-start.5
  20.8 7.2 %collective-permute-done.4 = bf16[64,1024]{1,0:T(8,128)(2,1)S(1)} collective-permute-done((bf16[64,1024]{1,0:T(8,128)(2,1)S(1)}, bf16[64,1024]{1,0:T(8,128)(2,1)S(1)}, u32[]{:S(2)}, u32[]{:S(2)}) %collective-permute-start.4) | collective-permute-done | bytes 131104 | tf_op jit(solution)/shard_map/ppermute | solution.py:722
  28.1 1.5 collective-permute-start.2
  31.5 5.0 %collective-permute-done.1 = bf16[64,1024]{1,0:T(8,128)(2,1)} collective-permute-done((bf16[64,1024]{1,0:T(8,128)(2,1)S(1)}, bf16[64,1024]{1,0:T(8,128)(2,1)}, u32[]{:S(2)}, u32[]{:S(2)}) %collective-permute-start.1) | collective-permute-done | bytes 131104 | tf_op jit(solution)/shard_map/ppermute | solution.py:722
  36.5 2.6 collective-permute-done.2
  39.1 1.1 pad_maximum_fusion.6
  43.5 2.8 collective-permute-start.12
  46.4 1.2 collective-permute-start.10
  48.5 1.5 collective-permute-start.8
  50.0 5.3 %collective-permute-done.10 = f32[1,3072]{1,0:T(1,128)S(1)} collective-permute-done((f32[1,3072]{1,0:T(1,128)S(1)}, f32[1,3072]{1,0:T(1,128)S(1)}, u32[]{:S(2)}, u32[]{:S(2)}) %collective-permute-start.10) | collective-permute-done | bytes 12320 | tf_op jit(solution)/shard_map/ppermute | solution.py:722
  55.9 12.7 %collective-permute-done.9 = bf16[4,64,1024]{2,1,0:T(8,128)(2,1)S(1)} collective-permute-done((bf16[4,64,1024]{2,1,0:T(8,128)(2,1)S(1)}, bf16[4,64,1024]{2,1,0:T(8,128)(2,1)S(1)}, u32[]{:S(2)}, u32[]{:S(2)}) %collective-permute-start.9) | collective-permute-done | bytes 524320 | tf_op jit(solution)/shard_map/ppermute | solution.py:722
  68.7 1.1 pad_maximum_fusion.1.p0
  71.0 1.7 collective-permute-start.14
  73.2 4.0 shard_map.295
  78.2 1.1 maximum_select_fusion.4
  79.4 1.2 maximum_select_fusion.2.b_ref.a_ref
  80.5 22.4 %collective-permute-done.13.p1 = bf16[8,64,1024]{2,1,0:T(8,128)(2,1)} collective-permute-done((bf16[8,64,1024]{2,1,0:T(8,128)(2,1)}, bf16[8,64,1024]{2,1,0:T(8,128)(2,1)}, u32[]{:S(2)}, u32[]{:S(2)}) %collective-permute-start.13) | collective-permute-done | bytes 1048608 | tf_op jit(solution)/shard_map/ppermute | solution.py:722
  103.0 7.2 %collective-permute-done.14.r1 = bf16[8,64,1024]{2,1,0:T(8,128)(2,1)S(1)} collective-permute-done((bf16[8,64,1024]{2,1,0:T(8,128)(2,1)S(1)}, bf16[8,64,1024]{2,1,0:T(8,128)(2,1)S(1)}, u32[]{:S(2)}, u32[]{:S(2)}) %collective-permute-start.14) | collective-permute-done | bytes 1048608 | tf_op jit(solution)/shard_map/ppermute | solution.py:722
  110.8 2.2 copy.49
  118.9 16.9 %shard_map.296 = (bf16[912,1024]{1,0:T(8,128)(2,1)}, bf16[912,1024]{1,0:T(8,128)(2,1)}, bf16[912,384]{1,0:T(8,128)(2,1)}, bf16[3,912,1024]{2,1,0:T(8,128)(2,1)},...) custom-call(s32[4]{0:T(128)} %pad_add_fusion.place, bf16[912,512]{1,0:T(8,128)(2,1)} %get-tuple-element.113.own_ref, ...), custom_call_target="tpu_custom_call" | custom-call | tf_op jit(solution)/shard_map/pallas_call | solution.py:859
  137.4 1.8 collective-permute-start.24
  139.2 3.2 collective-permute-start.22
  143.3 18.1 %shard_map.297 = (bf16[608,1024]{1,0:T(8,128)(2,1)}, bf16[16,608,608]{2,1,0:T(8,128)(2,1)}) custom-call(bf16[3,912,1024]{2,1,0:T(8,128)(2,1)} %get-tuple-element.139.q_ref.k_ref.v_ref, bf16[3,912,1024]{2,1,0:T(8,128)(2,1)} %get-tuple-element.139.q_ref.k_ref.v_ref, bf16[3,912,1024]{2,1,0:T(8,128)(2,1)} %get-tuple-element.139.q_ref.k_ref.v_ref, ...), custom_call_target="tpu_custom_call" | custom-call | tf_op jit(solution)/shard_map/pallas_call | solution.py:893
  162.3 10.2 %shard_map.298 = (bf16[304,512]{1,0:T(8,128)(2,1)}, bf16[304,512]{1,0:T(8,128)(2,1)}, bf16[8,608,608]{2,1,0:T(8,128)(2,1)}) custom-call(bf16[3,304,512]{2,1,0:T(8,128)(2,1)} %get-tuple-element.144.mine_ref, bf16[3,304,512]{2,1,0:T(8,128)(2,1)} %copy-done.7, bf16[608,128]{1,0:T(8,128)(2,1)} %broadcast_in_dim.71.mask_ref), custom_call_target="tpu_custom_call" | custom-call | tf_op jit(solution)/shard_map/pallas_call | solution.py:901
  172.5 12.8 %collective-permute-done.22.bup_near.adn_near = bf16[64,4096]{1,0:T(8,128)(2,1)S(1)} collective-permute-done((bf16[64,4096]{1,0:T(8,128)(2,1)S(1)}, bf16[64,4096]{1,0:T(8,128)(2,1)S(1)}, u32[]{:S(2)}, u32[]{:S(2)}) %collective-permute-start.22) | collective-permute-done | bytes 524320 | tf_op jit(solution)/shard_map/ppermute | solution.py:722
  185.4 1.2 pad_maximum_fusion.bup_own.adn_own
  187.3 10.6 %shard_map.299 = (f32[912,1024]{1,0:T(8,128)}, bf16[912,1024]{1,0:T(8,128)(2,1)}, bf16[912,128]{1,0:T(8,128)(2,1)}, bf16[912,128]{1,0:T(8,128)(2,1)}) custom-call(s32[4]{0:T(128)} %pad_add_fusion.place, bf16[608,1024]{1,0:T(8,128)(2,1)} %get-tuple-element.143.own_ref.att_ref, bf16[304,512]{1,0:T(8,128)(2,1)} %get-tuple-element.146.keep_ref.att_keep, ...), custom_call_target="tpu_custom_call" | custom-call | tf_op jit(solution)/shard_map/pallas_call | solution.py:915
  198.7 61.2 %shard_map.300 = (bf16[912,512]{1,0:T(8,128)(2,1)}, bf16[912,512]{1,0:T(8,128)(2,1)}, bf16[912,512]{1,0:T(8,128)(2,1)}, f32[912,1024]{1,0:T(8,128)}, bf16[912,10...) custom-call(s32[4]{0:T(128)} %pad_add_fusion.place, ...), custom_call_target="tpu_custom_call" | custom-call | tf_op jit(solution)/shard_map/pallas_call | solution.py:951
  260.4 2.9 collective-permute-done.26
  263.3 1.6 add_convert_fusion
  264.9 8.5 %shard_map.301 = (bf16[608,1024]{1,0:T(8,128)(2,1)}, bf16[304,512]{1,0:T(8,128)(2,1)}, bf16[304,512]{1,0:T(8,128)(2,1)}, bf16[2,64,1024]{2,1,0:T(8,128)(2,1)}, bf16[2,64,1024]{2,1,0:T(8,128)(2,1)}) custom-call(s32[4]{0:T(128)} %pad_add_fusion.place, bf16[912,1024]{1,0:T(8,128)(2,1)} %get-tuple-element.164.g_ref, ...), custom_call_target="tpu_custom_call" | custom-call | tf_op jit(solution)/shard_map/pallas_call | solution.py:996
  274.0 1.6 collective-permute-start.29
  276.6 1.2 collective-permute-start.30
  277.8 10.0 %shard_map.302 = (bf16[3,304,512]{2,1,0:T(8,128)(2,1)}, bf16[3,304,512]{2,1,0:T(8,128)(2,1)}) custom-call(bf16[3,304,512]{2,1,0:T(8,128)(2,1)} %get-tuple-element.144.mine_ref, bf16[3,304,512]{2,1,0:T(8,128)(2,1)} %copy-done.7, bf16[8,608,608]{2,1,0:T(8,128)(2,1)} %get-tuple-element.167.p_ref, bf16[304,512]{1,0:T(8,128)(2,1)} %get-tuple-element.146.keep_ref.att_keep, ...), custom_call_target="tpu_custom_call" | custom-call | tf_op jit(solution)/shard_map/pallas_call | solution.py:1027
  287.9 6.0 %collective-permute-done.30 = bf16[2,32,1024]{2,1,0:T(8,128)(2,1)S(1)} collective-permute-done((bf16[2,32,1024]{2,1,0:T(8,128)(2,1)S(1)}, bf16[2,32,1024]{2,1,0:T(8,128)(2,1)S(1)}, u32[]{:S(2)}, u32[]{:S(2)}) %collective-permute-start.30) | collective-permute-done | bytes 131104 | tf_op jit(solution)/shard_map/ppermute | solution.py:722
  294.4 17.9 %shard_map.303.own_ref = bf16[3,608,1024]{2,1,0:T(8,128)(2,1)} custom-call(bf16[3,912,1024]{2,1,0:T(8,128)(2,1)} %get-tuple-element.139.q_ref.k_ref.v_ref, bf16[3,912,1024]{2,1,0:T(8,128)(2,1)} %get-tuple-element.139.q_ref.k_ref.v_ref, bf16[3,912,1024]{2,1,0:T(8,128)(2,1)} %get-tuple-element.139.q_ref.k_ref.v_ref, ...), custom_call_target="tpu_custom_call" | custom-call | tf_op jit(solution)/shard_map/pallas_call | solution.py:1045
  312.4 1.5 collective-permute-start.34
  314.9 8.6 %shard_map.304 = (bf16[912,384]{1,0:T(8,128)(2,1)}, bf16[2,2,3,64,512]{4,3,2,1,0:T(8,128)(2,1)}, bf16[2,2,3,64,512]{4,3,2,1,0:T(8,128)(2,1)}) custom-call(s32[4]{0:T(128)} %pad_add_fusion.place, bf16[3,608,1024]{2,1,0:T(8,128)(2,1)} %shard_map.303.own_ref, bf16[3,304,512]{2,1,0:T(8,128)(2,1)} %get-tuple-element.181.keep_ref, bf16[3,304,512]{2,1,0:T(8,128)(2,1)} %copy-done.8, ...), custom_call_target="tpu_custom_call" | custom-call | tf_op jit(solution)/shard_map/pallas_call | solution.py:1058
  324.1 1.9 collective-permute-done.33
  326.0 1.4 add_convert_fusion.1
  328.2 1.5 collective-permute-start.35
  329.7 2.4 collective-permute-start.38
  332.1 1.9 collective-permute-start.36
  334.7 15.4 %shard_map.305 = (bf16[912,512]{1,0:T(8,128)(2,1)}, bf16[912,512]{1,0:T(8,128)(2,1)}, bf16[912,512]{1,0:T(8,128)(2,1)}) custom-call(s32[4]{0:T(128)} %pad_add_fusion.place, bf16[3,608,1024]{2,1,0:T(8,128)(2,1)} %shard_map.303.own_ref, bf16[3,304,512]{2,1,0:T(8,128)(2,1)} %get-tuple-element.181.keep_ref, bf16[3,304,512]{2,1,0:T(8,128)(2,1)} %copy-done.8, ...), custom_call_target="tpu_custom_call" | custom-call | tf_op jit(solution)/shard_map/pallas_call | solution.py:1074
  350.1 1.1 fusion.1
  351.4 2.7 collective-permute-done.36.near_ref
  354.1 3.8 collective-permute-start.40
  358.0 3.8 shard_map.306
  361.9 2.7 collective-permute-done.39
  367.3 3.6 collective-permute-done.41
  371.6 5.0 %collective-permute-done.45 = bf16[32,7680]{1,0:T(8,128)(2,1)S(1)} collective-permute-done((bf16[32,7680]{1,0:T(8,128)(2,1)S(1)}, bf16[32,7680]{1,0:T(8,128)(2,1)S(1)}, u32[]{:S(2)}, u32[]{:S(2)}) %collective-permute-start.45) | collective-permute-done | bytes 491552 | tf_op jit(solution)/shard_map/ppermute | solution.py:722
  376.7 4.0 collective-permute-done.42
  380.7 5.9 %collective-permute-done.43.near_ref = bf16[912,512]{1,0:T(8,128)(2,1)S(1)} collective-permute-done((bf16[912,512]{1,0:T(8,128)(2,1)}, bf16[912,512]{1,0:T(8,128)(2,1)S(1)}, u32[]{:S(2)}, u32[]{:S(2)}) %collective-permute-start.43) | collective-permute-done | bytes 933920 | tf_op jit(solution)/shard_map/ppermute | solution.py:722
  386.7 1.5 collective-permute-start.48
  388.2 1.5 collective-permute-start.46
  389.7 4.4 %shard_map.307 = f32[1731,512]{1,0:T(8,128)} custom-call(s32[4]{0:T(128)} %pad_add_fusion.place, bf16[912,512]{1,0:T(8,128)(2,1)} %get-tuple-element.209.own_ref, bf16[912,512]{1,0:T(8,128)(2,1)} %copy-done.18, bf16[912,512]{1,0:T(8,128)(2,1)} %copy-done.19), custom_call_target="tpu_custom_call" | custom-call | tf_op jit(solution)/shard_map/pallas_call | solution.py:751
  396.3 2.8 collective-permute-start.47
  399.5 4.4 %collective-permute-done.47 = bf16[1,192,512]{2,1,0:T(8,128)(2,1)S(1)} collective-permute-done((bf16[1,192,512]{2,1,0:T(8,128)(2,1)S(1)}, bf16[1,192,512]{2,1,0:T(8,128)(2,1)S(1)}, u32[]{:S(2)}, u32[]{:S(2)}) %collective-permute-start.47) | collective-permute-done | bytes 196640 | tf_op jit(solution)/shard_map/ppermute | solution.py:722
  406.3 2.7 slice_bitcast_fusion
  409.0 1.3 copy.57
  414.0 1.2 maximum_convert_fusion
  (202 shorter events, 40.7 us)
Async XLA Ops:
  7.2 22.4 %copy-start.23 = (bf16[2048,64]{0,1:T(8,128)(2,1)S(1)}, bf16[2048,64]{0,1:T(8,128)(2,1)}, u32[]{:S(2)}) copy-start(bf16[2048,64]{0,1:T(8,128)(2,1)} %param.35) | copy-start | bytes 786436
  7.2 22.4 %copy-start.24 = (bf16[64,2048]{1,0:T(8,128)(2,1)S(1)}, bf16[64,2048]{1,0:T(8,128)(2,1)}, u32[]{:S(2)}) copy-start(bf16[64,2048]{1,0:T(8,128)(2,1)} %param.33) | copy-start | bytes 786436
  7.2 190.8 %all-gather.3.cloned.1.call-start = ((), (), s32[]{:S(2)}) async-start(), calls=%async_computation | async-start | bytes 17301504 | tf_op jit(solution)/shard_map/all_gather | solution.py:788
  11.9 28.4 %collective-permute-start.6 = (bf16[912,512]{1,0:T(8,128)(2,1)}, bf16[912,512]{1,0:T(8,128)(2,1)S(1)}, u32[]{:S(2)}, u32[]{:S(2)}) collective-permute-start(bf16[912,512]{1,0:T(8,128)(2,1)} %get-tuple-element.118), channel_id=1, source_target_pairs={{0,2},{1,0},{2,3},{3,1},{4,6},{5,4},{6,7},{7,5},{8,10},{9,8},{10,1... | collective-permute-start | bytes 2801672 | tf_op jit(solution)/shard_map/ppermute | solution.py:722
  12.4 27.9 %collective-permute-start.7 = (bf16[912,512]{1,0:T(8,128)(2,1)}, bf16[912,512]{1,0:T(8,128)(2,1)S(1)}, u32[]{:S(2)}, u32[]{:S(2)}) collective-permute-start(bf16[912,512]{1,0:T(8,128)(2,1)} %get-tuple-element.119), channel_id=1, source_target_pairs={{1,2},{2,1},{5,6},{6,5},{9,10},{10,9},{13,14},{14,13},{17,18},{18,... | collective-permute-start | bytes 2801672 | tf_op jit(solution)/shard_map/ppermute | solution.py:722
  13.2 28.1 %copy-start.21 = (bf16[3,128,512]{2,1,0:T(8,128)(2,1)S(1)}, bf16[3,128,512]{2,1,0:T(8,128)(2,1)}, u32[]{:S(2)}) copy-start(bf16[3,128,512]{2,1,0:T(8,128)(2,1)} %param.39) | copy-start | bytes 1179652
  13.2 7.7 %collective-permute-start.3 = (bf16[64,1024]{1,0:T(8,128)(2,1)S(1)}, bf16[64,1024]{1,0:T(8,128)(2,1)S(1)}, u32[]{:S(2)}, u32[]{:S(2)}) collective-permute-start(bf16[64,1024]{1,0:T(8,128)(2,1)S(1)} %get-tuple-element.250), channel_id=1, source_target_pairs={{0,8},{1,9},{2,10},{3,11},{4,12},{5,13},{6,14},{7,15},{8,16},{9,17... | collective-permute-start | bytes 393224 | tf_op jit(solution)/shard_map/ppermute | solution.py:722
  15.8 12.2 %collective-permute-start.4 = (bf16[64,1024]{1,0:T(8,128)(2,1)S(1)}, bf16[64,1024]{1,0:T(8,128)(2,1)S(1)}, u32[]{:S(2)}, u32[]{:S(2)}) collective-permute-start(bf16[64,1024]{1,0:T(8,128)(2,1)S(1)} %get-tuple-element.250), channel_id=1, source_target_pairs={{0,16},{1,17},{2,18},{3,19},{4,20},{5,21},{6,22},{7,23},{8,24},{9,... | collective-permute-start | bytes 393224 | tf_op jit(solution)/shard_map/ppermute | solution.py:722
  18.4 9.7 %collective-permute-start.5 = (bf16[64,1024]{1,0:T(8,128)(2,1)S(1)}, bf16[64,1024]{1,0:T(8,128)(2,1)S(1)}, u32[]{:S(2)}, u32[]{:S(2)}) collective-permute-start(bf16[64,1024]{1,0:T(8,128)(2,1)S(1)} %get-tuple-element.250), channel_id=1, source_target_pairs={{0,24},{1,25},{2,26},{3,27},{4,28},{5,29},{6,30},{7,31},{8,0},{9,1... | collective-permute-start | bytes 393224 | tf_op jit(solution)/shard_map/ppermute | solution.py:722
  20.8 9.6 %copy-start.28 = (bf16[64,1024]{1,0:T(8,128)(2,1)}, bf16[64,1024]{1,0:T(8,128)(2,1)S(1)}, u32[]{:S(2)}) copy-start(bf16[64,1024]{1,0:T(8,128)(2,1)S(1)} %collective-permute-done.3) | copy-start | bytes 393220
  20.8 10.7 %collective-permute-start = (bf16[64,1024]{1,0:T(8,128)(2,1)S(1)}, bf16[64,1024]{1,0:T(8,128)(2,1)}, u32[]{:S(2)}, u32[]{:S(2)}) collective-permute-start(bf16[64,1024]{1,0:T(8,128)(2,1)S(1)} %get-tuple-element.252), channel_id=1, source_target_pairs={{0,8},{1,9},{2,10},{3,11},{4,12},{5,13},{6,14},{7,15},{8,16},{9,17... | collective-permute-start | bytes 393224 | tf_op jit(solution)/shard_map/ppermute | solution.py:722
  28.0 8.5 %collective-permute-start.1 = (bf16[64,1024]{1,0:T(8,128)(2,1)S(1)}, bf16[64,1024]{1,0:T(8,128)(2,1)}, u32[]{:S(2)}, u32[]{:S(2)}) collective-permute-start(bf16[64,1024]{1,0:T(8,128)(2,1)S(1)} %get-tuple-element.252), channel_id=1, source_target_pairs={{0,16},{1,17},{2,18},{3,19},{4,20},{5,21},{6,22},{7,23},{8,24},{9,... | collective-permute-start | bytes 393224 | tf_op jit(solution)/shard_map/ppermute | solution.py:722
  28.1 11.1 %collective-permute-start.2 = (bf16[64,1024]{1,0:T(8,128)(2,1)S(1)}, bf16[64,1024]{1,0:T(8,128)(2,1)}, u32[]{:S(2)}, u32[]{:S(2)}) collective-permute-start(bf16[64,1024]{1,0:T(8,128)(2,1)S(1)} %get-tuple-element.252), channel_id=1, source_target_pairs={{0,24},{1,25},{2,26},{3,27},{4,28},{5,29},{6,30},{7,31},{8,0},{9,1... | collective-permute-start | bytes 393224 | tf_op jit(solution)/shard_map/ppermute | solution.py:722
  42.8 27.1 %copy-start.13 = (bf16[512,128]{0,1:T(8,128)(2,1)}, bf16[512,128]{0,1:T(8,128)(2,1)S(1)}, u32[]{:S(2)}) copy-start(bf16[512,128]{0,1:T(8,128)(2,1)S(1)} %copy.47) | copy-start | bytes 393220
  43.5 26.3 %collective-permute-start.12 = (bf16[64,2048]{1,0:T(8,128)(2,1)}, bf16[64,2048]{1,0:T(8,128)(2,1)S(1)}, u32[]{:S(2)}, u32[]{:S(2)}) collective-permute-start(bf16[64,2048]{1,0:T(8,128)(2,1)} %fusion.9), channel_id=1, source_target_pairs={{0,1},{1,0},{2,3},{3,2},{4,5},{5,4},{6,7},{7,6},{8,9},{9,8},{10,11... | collective-permute-start | bytes 786440 | tf_op jit(solution)/shard_map/ppermute | solution.py:722
  46.3 3.6 collective-permute-start.11
  46.4 8.9 %collective-permute-start.10 = (f32[1,3072]{1,0:T(1,128)S(1)}, f32[1,3072]{1,0:T(1,128)S(1)}, u32[]{:S(2)}, u32[]{:S(2)}) collective-permute-start(f32[1,3072]{1,0:T(1,128)S(1)} %bitcast.113), channel_id=1, source_target_pairs={{0,1},{1,0},{2,3},{3,2},{4,5},{5,4},{6,7},{7,6},{8,9},{9,8},{10,11... | collective-permute-start | bytes 36872 | tf_op jit(solution)/shard_map/ppermute | solution.py:722
  47.5 21.1 %collective-permute-start.9 = (bf16[4,64,1024]{2,1,0:T(8,128)(2,1)S(1)}, bf16[4,64,1024]{2,1,0:T(8,128)(2,1)S(1)}, u32[]{:S(2)}, u32[]{:S(2)}) collective-permute-start(bf16[4,64,1024]{2,1,0:T(8,128)(2,1)S(1)} %pad_maximum_fusion.7), channel_id=1, source_target_pairs={{0,1},{1,0},{2,3},{3,2},{4,5},{5,4},{6,7},{7,6},{8,9},{9,8},{10,11... | collective-permute-start | bytes 1572872 | tf_op jit(solution)/shard_map/ppermute | solution.py:722
  48.5 20.2 %collective-permute-start.8 = (bf16[4,64,1024]{2,1,0:T(8,128)(2,1)S(1)}, bf16[4,64,1024]{2,1,0:T(8,128)(2,1)S(1)}, u32[]{:S(2)}, u32[]{:S(2)}) collective-permute-start(bf16[4,64,1024]{2,1,0:T(8,128)(2,1)S(1)} %pad_maximum_fusion.6), channel_id=1, source_target_pairs={{0,4},{1,5},{2,6},{3,7},{4,0},{5,1},{6,2},{7,3},{8,12},{9,13},{10,... | collective-permute-start | bytes 1572872 | tf_op jit(solution)/shard_map/ppermute | solution.py:722
  68.7 9.5 %copy-start = (bf16[8,64,1024]{2,1,0:T(8,128)(2,1)}, bf16[8,64,1024]{2,1,0:T(8,128)(2,1)S(1)}, u32[]{:S(2)}) copy-start(bf16[8,64,1024]{2,1,0:T(8,128)(2,1)S(1)} %pad_maximum_fusion.2.r0) | copy-start | bytes 3145732
  69.9 33.1 %collective-permute-start.13 = (bf16[8,64,1024]{2,1,0:T(8,128)(2,1)}, bf16[8,64,1024]{2,1,0:T(8,128)(2,1)}, u32[]{:S(2)}, u32[]{:S(2)}) collective-permute-start(bf16[8,64,1024]{2,1,0:T(8,128)(2,1)} %pad_maximum_fusion.1.p0), channel_id=1, source_target_pairs={{0,1},{1,0},{2,3},{3,2},{4,5},{5,4},{6,7},{7,6},{8,9},{9,8},{10,11... | collective-permute-start | bytes 3145736 | tf_op jit(solution)/shard_map/ppermute | solution.py:722
  71.0 39.2 %collective-permute-start.14 = (bf16[8,64,1024]{2,1,0:T(8,128)(2,1)S(1)}, bf16[8,64,1024]{2,1,0:T(8,128)(2,1)S(1)}, u32[]{:S(2)}, u32[]{:S(2)}) collective-permute-start(bf16[8,64,1024]{2,1,0:T(8,128)(2,1)S(1)} %pad_maximum_fusion.2.r0), channel_id=1, source_target_pairs={{0,4},{1,5},{2,6},{3,7},{4,0},{5,1},{6,2},{7,3},{8,12},{9,13},{10,... | collective-permute-start | bytes 3145736 | tf_op jit(solution)/shard_map/ppermute | solution.py:722
  72.7 37.5 %collective-permute-start.15 = (bf16[8,64,1024]{2,1,0:T(8,128)(2,1)}, bf16[8,64,1024]{2,1,0:T(8,128)(2,1)}, u32[]{:S(2)}, u32[]{:S(2)}) collective-permute-start(bf16[8,64,1024]{2,1,0:T(8,128)(2,1)} %pad_maximum_fusion.1.p0), channel_id=1, source_target_pairs={{0,2},{1,3},{2,0},{3,1},{4,6},{5,7},{6,4},{7,5},{8,10},{9,11},{10,... | collective-permute-start | bytes 3145736 | tf_op jit(solution)/shard_map/ppermute | solution.py:722
  72.7 37.5 %collective-permute-start.16 = (bf16[8,64,1024]{2,1,0:T(8,128)(2,1)S(1)}, bf16[8,64,1024]{2,1,0:T(8,128)(2,1)S(1)}, u32[]{:S(2)}, u32[]{:S(2)}) collective-permute-start(bf16[8,64,1024]{2,1,0:T(8,128)(2,1)S(1)} %pad_maximum_fusion.2.r0), channel_id=1, source_target_pairs={{0,2},{1,3},{2,0},{3,1},{4,6},{5,7},{6,4},{7,5},{8,10},{9,11},{10,... | collective-permute-start | bytes 3145736 | tf_op jit(solution)/shard_map/ppermute | solution.py:722
  73.2 5.0 %collective-permute-start.17 = (bf16[64,2048]{1,0:T(8,128)(2,1)}, bf16[64,2048]{1,0:T(8,128)(2,1)}, u32[]{:S(2)}, u32[]{:S(2)}) collective-permute-start(bf16[64,2048]{1,0:T(8,128)(2,1)} %copy-done.25), channel_id=1, source_target_pairs={{0,2},{1,3},{2,0},{3,1},{4,6},{5,7},{6,4},{7,5},{8,10},{9,11},{10,... | collective-permute-start | bytes 786440 | tf_op jit(solution)/shard_map/ppermute | solution.py:722
  110.2 7.8 %copy-start.1 = (bf16[8,64,1024]{2,1,0:T(8,128)(2,1)}, bf16[8,64,1024]{2,1,0:T(8,128)(2,1)S(1)}, u32[]{:S(2)}) copy-start(bf16[8,64,1024]{2,1,0:T(8,128)(2,1)S(1)} %collective-permute-done.14.r1) | copy-start | bytes 3145732
  110.2 7.8 %collective-permute-start.18 = (bf16[8,64,1024]{2,1,0:T(8,128)(2,1)}, bf16[8,64,1024]{2,1,0:T(8,128)(2,1)}, u32[]{:S(2)}, u32[]{:S(2)}) collective-permute-start(bf16[8,64,1024]{2,1,0:T(8,128)(2,1)} %collective-permute-done.13.p1), channel_id=1, source_target_pairs={{0,2},{1,3},{2,0},{3,1},{4,6},{5,7},{6,4},{7,5},{8,10},{9,11},{10,... | collective-permute-start | bytes 3145736 | tf_op jit(solution)/shard_map/ppermute | solution.py:722
  110.3 7.7 %collective-permute-start.19 = (bf16[8,64,1024]{2,1,0:T(8,128)(2,1)S(1)}, bf16[8,64,1024]{2,1,0:T(8,128)(2,1)S(1)}, u32[]{:S(2)}, u32[]{:S(2)}) collective-permute-start(bf16[8,64,1024]{2,1,0:T(8,128)(2,1)S(1)} %collective-permute-done.14.r1), channel_id=1, source_target_pairs={{0,2},{1,3},{2,0},{3,1},{4,6},{5,7},{6,4},{7,5},{8,10},{9,11},{10,... | collective-permute-start | bytes 3145736 | tf_op jit(solution)/shard_map/ppermute | solution.py:722
  118.9 17.0 %copy-start.5 = (bf16[2048,128]{0,1:T(8,128)(2,1)S(1)}, bf16[2048,128]{0,1:T(8,128)(2,1)}, u32[]{:S(2)}) copy-start(bf16[2048,128]{0,1:T(8,128)(2,1)} %copy.49) | copy-start | bytes 1572868
  135.8 25.5 %collective-permute-start.20 = (bf16[3,304,512]{2,1,0:T(8,128)(2,1)}, bf16[3,304,512]{2,1,0:T(8,128)(2,1)S(1)}, u32[]{:S(2)}, u32[]{:S(2)}) collective-permute-start(bf16[3,304,512]{2,1,0:T(8,128)(2,1)} %get-tuple-element.141), channel_id=1, source_target_pairs={{0,2},{1,3},{2,0},{3,1},{4,6},{5,7},{6,4},{7,5},{8,10},{9,11},{10,... | collective-permute-start | bytes 2801672 | tf_op jit(solution)/shard_map/ppermute | solution.py:722
  136.9 48.4 %collective-permute-start.23 = (bf16[912,512]{1,0:T(8,128)(2,1)}, bf16[912,512]{1,0:T(8,128)(2,1)S(1)}, u32[]{:S(2)}, u32[]{:S(2)}) collective-permute-start(bf16[912,512]{1,0:T(8,128)(2,1)} %get-tuple-element.149), channel_id=1, source_target_pairs={{0,2},{1,0},{2,3},{3,1},{4,6},{5,4},{6,7},{7,5},{8,10},{9,8},{10,1... | collective-permute-start | bytes 2801672 | tf_op jit(solution)/shard_map/ppermute | solution.py:722
  137.4 47.9 %collective-permute-start.24 = (bf16[912,512]{1,0:T(8,128)(2,1)}, bf16[912,512]{1,0:T(8,128)(2,1)}, u32[]{:S(2)}, u32[]{:S(2)}) collective-permute-start(bf16[912,512]{1,0:T(8,128)(2,1)} %get-tuple-element.150), channel_id=1, source_target_pairs={{1,2},{2,1},{5,6},{6,5},{9,10},{10,9},{13,14},{14,13},{17,18},{18,... | collective-permute-start | bytes 2801672 | tf_op jit(solution)/shard_map/ppermute | solution.py:722
  139.2 46.1 %collective-permute-start.22 = (bf16[64,4096]{1,0:T(8,128)(2,1)S(1)}, bf16[64,4096]{1,0:T(8,128)(2,1)S(1)}, u32[]{:S(2)}, u32[]{:S(2)}) collective-permute-start(bf16[64,4096]{1,0:T(8,128)(2,1)S(1)} %fusion.4), channel_id=1, source_target_pairs={{0,1},{1,0},{2,3},{3,2},{4,5},{5,4},{6,7},{7,6},{8,9},{9,8},{10,11... | collective-permute-start | bytes 1572872 | tf_op jit(solution)/shard_map/ppermute | solution.py:722
  161.3 24.1 %copy-start.6 = (bf16[2048,128]{0,1:T(8,128)(2,1)S(1)}, bf16[2048,128]{0,1:T(8,128)(2,1)}, u32[]{:S(2)}) copy-start(bf16[2048,128]{0,1:T(8,128)(2,1)} %copy.49) | copy-start | bytes 1572868
  161.3 24.1 %copy-start.11 = (bf16[128,2048]{1,0:T(8,128)(2,1)S(1)}, bf16[128,2048]{1,0:T(8,128)(2,1)}, u32[]{:S(2)}) copy-start(bf16[128,2048]{1,0:T(8,128)(2,1)} %param.43) | copy-start | bytes 1572868
  162.3 24.3 %copy-start.31 = (f32[2,3072]{1,0:T(2,128)S(1)}, f32[2,3072]{1,0:T(2,128)}, u32[]{:S(2)}) copy-start(f32[2,3072]{1,0:T(2,128)} %maximum_select_fusion.10) | copy-start | bytes 73732
  172.5 12.8 %collective-permute-start.21 = (bf16[304,512]{1,0:T(8,128)(2,1)}, bf16[304,512]{1,0:T(8,128)(2,1)S(1)}, u32[]{:S(2)}, u32[]{:S(2)}) collective-permute-start(bf16[304,512]{1,0:T(8,128)(2,1)} %get-tuple-element.147.att_send), channel_id=1, source_target_pairs={{0,2},{1,3},{2,0},{3,1},{4,6},{5,7},{6,4},{7,5},{8,10},{9,11},{10,... | collective-permute-start | bytes 933896 | tf_op jit(solution)/shard_map/ppermute | solution.py:722
  185.3 12.6 %copy-start.9 = (bf16[64,4096]{1,0:T(8,128)(2,1)}, bf16[64,4096]{1,0:T(8,128)(2,1)S(1)}, u32[]{:S(2)}) copy-start(bf16[64,4096]{1,0:T(8,128)(2,1)S(1)} %collective-permute-done.22.bup_near.adn_near) | copy-start | bytes 1572868
  185.3 12.7 %copy-start.20 = (bf16[912,512]{1,0:T(8,128)(2,1)}, bf16[912,512]{1,0:T(8,128)(2,1)S(1)}, u32[]{:S(2)}) copy-start(bf16[912,512]{1,0:T(8,128)(2,1)S(1)} %collective-permute-done.23.gnear_ref) | copy-start | bytes 2801668
  185.3 12.6 %collective-permute-start.25 = (bf16[64,4096]{1,0:T(8,128)(2,1)S(1)}, bf16[64,4096]{1,0:T(8,128)(2,1)S(1)}, u32[]{:S(2)}, u32[]{:S(2)}) collective-permute-start(bf16[64,4096]{1,0:T(8,128)(2,1)S(1)} %collective-permute-done.22.bup_near.adn_near), channel_id=1, source_target_pairs={{0,2},{1,3},{2,0},{3,1},{4,6},{5,7},{6,4},{7,5},{8,10},{9,11},{10,... | collective-permute-start | bytes 1572872 | tf_op jit(solution)/shard_map/ppermute | solution.py:722
  260.0 3.3 collective-permute-start.26
  273.4 2.2 collective-permute-start.28
  273.8 2.8 collective-permute-start.27
  274.0 19.9 %collective-permute-start.29 = (bf16[2,32,5120]{2,1,0:T(8,128)(2,1)S(1)}, bf16[2,32,5120]{2,1,0:T(8,128)(2,1)S(1)}, u32[]{:S(2)}, u32[]{:S(2)}) collective-permute-start(bf16[2,32,5120]{2,1,0:T(8,128)(2,1)S(1)} %constant_dynamic-slice_fusion.1), channel_id=1, source_target_pairs={{0,4},{1,5},{2,6},{3,7},{4,0},{5,1},{6,2},{7,3},{8,12},{9,13},{10,... | collective-permute-start | bytes 1966088 | tf_op jit(solution)/shard_map/ppermute | solution.py:722
  276.6 17.2 %collective-permute-start.30 = (bf16[2,32,1024]{2,1,0:T(8,128)(2,1)S(1)}, bf16[2,32,1024]{2,1,0:T(8,128)(2,1)S(1)}, u32[]{:S(2)}, u32[]{:S(2)}) collective-permute-start(bf16[2,32,1024]{2,1,0:T(8,128)(2,1)S(1)} %constant_dynamic-slice_fusion), channel_id=1, source_target_pairs={{0,4},{1,5},{2,6},{3,7},{4,0},{5,1},{6,2},{7,3},{8,12},{9,13},{10,... | collective-permute-start | bytes 393224 | tf_op jit(solution)/shard_map/ppermute | solution.py:722
  294.2 18.1 %collective-permute-start.31 = (bf16[32,6144]{1,0:T(8,128)(2,1)S(1)}, bf16[32,6144]{1,0:T(8,128)(2,1)S(1)}, u32[]{:S(2)}, u32[]{:S(2)}) collective-permute-start(bf16[32,6144]{1,0:T(8,128)(2,1)S(1)} %select_bitcast_fusion), channel_id=1, source_target_pairs={{0,1},{1,0},{2,3},{3,2},{4,5},{5,4},{6,7},{7,6},{8,9},{9,8},{10,11... | collective-permute-start | bytes 1179656 | tf_op jit(solution)/shard_map/ppermute | solution.py:722
  294.3 19.6 %collective-permute-start.32 = (bf16[3,304,512]{2,1,0:T(8,128)(2,1)}, bf16[3,304,512]{2,1,0:T(8,128)(2,1)S(1)}, u32[]{:S(2)}, u32[]{:S(2)}) collective-permute-start(bf16[3,304,512]{2,1,0:T(8,128)(2,1)} %get-tuple-element.182), channel_id=1, source_target_pairs={{0,2},{1,3},{2,0},{3,1},{4,6},{5,7},{6,4},{7,5},{8,10},{9,11},{10,... | collective-permute-start | bytes 2801672 | tf_op jit(solution)/shard_map/ppermute | solution.py:722
  312.4 11.6 %collective-permute-start.34 = (bf16[32,6144]{1,0:T(8,128)(2,1)S(1)}, bf16[32,6144]{1,0:T(8,128)(2,1)S(1)}, u32[]{:S(2)}, u32[]{:S(2)}) collective-permute-start(bf16[32,6144]{1,0:T(8,128)(2,1)S(1)} %fusion.2), channel_id=1, source_target_pairs={{0,8},{1,9},{2,10},{3,11},{4,12},{5,13},{6,14},{7,15},{8,0},{9,1},... | collective-permute-start | bytes 1179656 | tf_op jit(solution)/shard_map/ppermute | solution.py:722
  323.5 2.5 collective-permute-start.33
  328.2 21.9 %collective-permute-start.35 = (bf16[2,192,512]{2,1,0:T(8,128)(2,1)}, bf16[2,192,512]{2,1,0:T(8,128)(2,1)}, u32[]{:S(2)}, u32[]{:S(2)}) collective-permute-start(bf16[2,192,512]{2,1,0:T(8,128)(2,1)} %fusion.8), channel_id=1, source_target_pairs={{0,4},{1,5},{2,6},{3,7},{4,0},{5,1},{6,2},{7,3},{8,12},{9,13},{10,... | collective-permute-start | bytes 1179656 | tf_op jit(solution)/shard_map/ppermute | solution.py:722
  329.7 21.6 %collective-permute-start.38 = (bf16[32,6144]{1,0:T(8,128)(2,1)S(1)}, bf16[32,6144]{1,0:T(8,128)(2,1)S(1)}, u32[]{:S(2)}, u32[]{:S(2)}) collective-permute-start(bf16[32,6144]{1,0:T(8,128)(2,1)S(1)} %add_convert_fusion.4), channel_id=1, source_target_pairs={{0,16},{1,17},{2,18},{3,19},{4,20},{5,21},{6,22},{7,23},{8,24},{9,... | collective-permute-start | bytes 1179656 | tf_op jit(solution)/shard_map/ppermute | solution.py:722
  332.1 22.0 %collective-permute-start.36 = (bf16[912,512]{1,0:T(8,128)(2,1)}, bf16[912,512]{1,0:T(8,128)(2,1)S(1)}, u32[]{:S(2)}, u32[]{:S(2)}) collective-permute-start(bf16[912,512]{1,0:T(8,128)(2,1)} %get-tuple-element.195), channel_id=1, source_target_pairs={{0,1},{1,3},{2,0},{3,2},{4,5},{5,7},{6,4},{7,6},{8,9},{9,11},{10,8... | collective-permute-start | bytes 2801672 | tf_op jit(solution)/shard_map/ppermute | solution.py:722
  334.0 20.1 %collective-permute-start.37 = (bf16[912,512]{1,0:T(8,128)(2,1)}, bf16[912,512]{1,0:T(8,128)(2,1)S(1)}, u32[]{:S(2)}, u32[]{:S(2)}) collective-permute-start(bf16[912,512]{1,0:T(8,128)(2,1)} %get-tuple-element.196), channel_id=1, source_target_pairs={{1,2},{2,1},{5,6},{6,5},{9,10},{10,9},{13,14},{14,13},{17,18},{18,... | collective-permute-start | bytes 2801672 | tf_op jit(solution)/shard_map/ppermute | solution.py:722
  354.1 7.7 %collective-permute-start.40 = (bf16[32,1536]{1,0:T(8,128)(2,1)S(1)}, bf16[32,1536]{1,0:T(8,128)(2,1)S(1)}, u32[]{:S(2)}, u32[]{:S(2)}) collective-permute-start(bf16[32,1536]{1,0:T(8,128)(2,1)S(1)} %pad_maximum_fusion.11), channel_id=1, source_target_pairs={{0,1},{1,0},{2,3},{3,2},{4,5},{5,4},{6,7},{7,6},{8,9},{9,8},{10,11... | collective-permute-start | bytes 294920 | tf_op jit(solution)/shard_map/ppermute | solution.py:722
  357.9 6.6 %collective-permute-start.39 = (bf16[192,512]{1,0:T(8,128)(2,1)S(1)}, bf16[192,512]{1,0:T(8,128)(2,1)S(1)}, u32[]{:S(2)}, u32[]{:S(2)}) collective-permute-start(bf16[192,512]{1,0:T(8,128)(2,1)S(1)} %select_bitcast_fusion.1), channel_id=1, source_target_pairs={{0,1},{1,0},{2,3},{3,2},{4,5},{5,4},{6,7},{7,6},{8,9},{9,8},{10,11... | collective-permute-start | bytes 589832 | tf_op jit(solution)/shard_map/ppermute | solution.py:722
  364.6 12.0 %collective-permute-start.45 = (bf16[32,7680]{1,0:T(8,128)(2,1)S(1)}, bf16[32,7680]{1,0:T(8,128)(2,1)S(1)}, u32[]{:S(2)}, u32[]{:S(2)}) collective-permute-start(bf16[32,7680]{1,0:T(8,128)(2,1)S(1)} %pad_maximum_fusion.9), channel_id=1, source_target_pairs={{0,4},{1,5},{2,6},{3,7},{4,0},{5,1},{6,2},{7,3},{8,12},{9,13},{10,... | collective-permute-start | bytes 1474568 | tf_op jit(solution)/shard_map/ppermute | solution.py:722
  365.2 5.7 %collective-permute-start.41 = (bf16[192,512]{1,0:T(8,128)(2,1)S(1)}, bf16[192,512]{1,0:T(8,128)(2,1)S(1)}, u32[]{:S(2)}, u32[]{:S(2)}) collective-permute-start(bf16[192,512]{1,0:T(8,128)(2,1)S(1)} %fusion.7), channel_id=1, source_target_pairs={{0,8},{1,9},{2,10},{3,11},{4,12},{5,13},{6,14},{7,15},{8,0},{9,1},... | collective-permute-start | bytes 589832 | tf_op jit(solution)/shard_map/ppermute | solution.py:722
  365.8 20.8 %collective-permute-start.43 = (bf16[912,512]{1,0:T(8,128)(2,1)}, bf16[912,512]{1,0:T(8,128)(2,1)S(1)}, u32[]{:S(2)}, u32[]{:S(2)}) collective-permute-start(bf16[912,512]{1,0:T(8,128)(2,1)} %get-tuple-element.205), channel_id=1, source_target_pairs={{0,1},{1,3},{2,0},{3,2},{4,5},{5,7},{6,4},{7,6},{8,9},{9,11},{10,8... | collective-permute-start | bytes 2801672 | tf_op jit(solution)/shard_map/ppermute | solution.py:722
  366.6 20.1 %collective-permute-start.44 = (bf16[912,512]{1,0:T(8,128)(2,1)}, bf16[912,512]{1,0:T(8,128)(2,1)S(1)}, u32[]{:S(2)}, u32[]{:S(2)}) collective-permute-start(bf16[912,512]{1,0:T(8,128)(2,1)} %get-tuple-element.206), channel_id=1, source_target_pairs={{1,2},{2,1},{5,6},{6,5},{9,10},{10,9},{13,14},{14,13},{17,18},{18,... | collective-permute-start | bytes 2801672 | tf_op jit(solution)/shard_map/ppermute | solution.py:722
  371.0 9.7 %collective-permute-start.42 = (bf16[192,512]{1,0:T(8,128)(2,1)S(1)}, bf16[192,512]{1,0:T(8,128)(2,1)S(1)}, u32[]{:S(2)}, u32[]{:S(2)}) collective-permute-start(bf16[192,512]{1,0:T(8,128)(2,1)S(1)} %add_convert_fusion.7), channel_id=1, source_target_pairs={{0,16},{1,17},{2,18},{3,19},{4,20},{5,21},{6,22},{7,23},{8,24},{9,... | collective-permute-start | bytes 589832 | tf_op jit(solution)/shard_map/ppermute | solution.py:722
  386.7 12.4 %collective-permute-start.48 = (bf16[64,7680]{1,0:T(8,128)(2,1)S(1)}, bf16[64,7680]{1,0:T(8,128)(2,1)S(1)}, u32[]{:S(2)}, u32[]{:S(2)}) collective-permute-start(bf16[64,7680]{1,0:T(8,128)(2,1)S(1)} %maximum_select_fusion.3), channel_id=1, source_target_pairs={{0,2},{1,3},{2,0},{3,1},{4,6},{5,7},{6,4},{7,5},{8,10},{9,11},{10,... | collective-permute-start | bytes 2949128 | tf_op jit(solution)/shard_map/ppermute | solution.py:722
  388.2 7.0 %collective-permute-start.46 = (bf16[192,512]{1,0:T(8,128)(2,1)S(1)}, bf16[192,512]{1,0:T(8,128)(2,1)}, u32[]{:S(2)}, u32[]{:S(2)}) collective-permute-start(bf16[192,512]{1,0:T(8,128)(2,1)S(1)} %add_convert_fusion.6), channel_id=1, source_target_pairs={{0,4},{1,5},{2,6},{3,7},{4,0},{5,1},{6,2},{7,3},{8,12},{9,13},{10,... | collective-permute-start | bytes 589832 | tf_op jit(solution)/shard_map/ppermute | solution.py:722
  396.3 7.6 %collective-permute-start.47 = (bf16[1,192,512]{2,1,0:T(8,128)(2,1)S(1)}, bf16[1,192,512]{2,1,0:T(8,128)(2,1)S(1)}, u32[]{:S(2)}, u32[]{:S(2)}) collective-permute-start(bf16[1,192,512]{2,1,0:T(8,128)(2,1)S(1)} %get-tuple-element.249), channel_id=1, source_target_pairs={{0,1},{1,0},{2,3},{3,2},{4,5},{5,4},{6,7},{7,6},{8,9},{9,8},{10,11... | collective-permute-start | bytes 589832 | tf_op jit(solution)/shard_map/ppermute | solution.py:722
  406.2 5.8 %collective-permute-start.49 = (bf16[3,3,64,512]{3,2,1,0:T(8,128)(2,1)S(1)}, bf16[3,3,64,512]{3,2,1,0:T(8,128)(2,1)S(1)}, u32[]{:S(2)}, u32[]{:S(2)}) collective-permute-start(bf16[3,3,64,512]{3,2,1,0:T(8,128)(2,1)S(1)} %bitcast.93), channel_id=1, source_target_pairs={{0,2},{1,3},{2,0},{3,1},{4,6},{5,7},{6,4},{7,5},{8,10},{9,11},{10,... | collective-permute-start | bytes 1769480 | tf_op jit(solution)/shard_map/ppermute | solution.py:722
  (23 other events, 81.5 us)
Sparse Core Ops, SparseCore 0:
  40.5 147.1 all-gather.2
